TPU v7x, 32 devices: a whole 2x2x4 slice. The times are simulated.
32 devices in a mesh: pix: 8 (over z, x), br: 4 (over y, core).
Axes of the slice: x: 2, y: 2, z: 4, core: 2. Of those that a mesh axis runs over, the one named last changes fastest.
Arguments:
- features: bfloat16 [192, 64, 2048], P('pix'), may hold values from -6 to 6
- branch_weight: bfloat16 [4, 2048, 512], P('br'), may hold values from -0.125 to 0.125
- branch_gain: float32 [4, 512], P('br'), may hold values from 0.5 to 1.5
- branch_shift: float32 [4, 512], P('br'), may hold values from -2 to 2
- trunk_weight: bfloat16 [4, 3, 3, 1024, 512], P('br'), may hold values from -0.03125 to 0.03125
- trunk_gain: float32 [512], replicated, may hold values from 0.5 to 1.5
- trunk_shift: float32 [512], replicated, may hold values from -2 to 2
- class_weight: bfloat16 [512, 150], replicated, may hold values from -0.25 to 0.25
- class_bias: float32 [150], replicated, may hold values from -2 to 2
- heights: int32 [16], replicated, may hold values from 1 to 96, as said below
- logit_grad: bfloat16 [192, 64, 150], P(('pix', 'br')), may hold values from -6 to 6
Outputs:
- logits: bfloat16 [192, 64, 150], P(('pix', 'br'))
- feature_grad: float32 [192, 64, 2048], P('pix', None, 'br')
- branch_weight_grad: float32 [4, 2048, 512], P('br', 'pix')
- branch_gain_grad: float32 [4, 512], P('br')
- branch_shift_grad: float32 [4, 512], P('br')
- trunk_weight_grad: float32 [4, 3, 3, 1024, 512], P('br', None, None, 'pix')
- trunk_gain_grad: float32 [512], P('br')
- trunk_shift_grad: float32 [512], P('br')
- class_weight_grad: float32 [512, 150], P('br')
- class_bias_grad: float32 [150], replicated
Inputs may be any that keep to these rules, and one draw needn't show every extreme that they name: The images' heights in canvas rows, top to bottom; every image spans all 64 columns and the heights sum to 192.
All inputs are finite; a program needn't handle non-finite values.
Results may differ from a plain program's by a relative error of at most 0.0077.
Values may be sent and summed in bfloat16 or wider, within the bound.
A program may use at most 256 MiB of HBM per device.

v0:
```python
import jax
import jax.numpy as jnp
from jax import lax
from jax.sharding import PartitionSpec as P

bin_sides = (1, 2, 3, 6)
norm_eps = 1e-05


def padded_2(cells, sides, width):
    for axis, dim in sides:
        count = lax.axis_size(axis)
        ends = count - 1
        head = lax.slice_in_dim(cells, 0, width, axis=dim)
        tail = lax.slice_in_dim(cells, cells.shape[dim] - width, cells.shape[dim], axis=dim)
        cells = jnp.concatenate(
            [
                lax.ppermute(tail, axis, [(i, (i + 1) % count) for i in range(ends)]),
                cells,
                lax.ppermute(head, axis, [((i + 1) % count, i) for i in range(ends)]),
            ],
            axis=dim,
        )
    return cells


def activate(value):
    return jax.nn.gelu(value, approximate=True)


def gelu_slope(value):
    unused, pull = jax.vjp(activate, value)
    return pull(jnp.ones_like(value))[0]


def image_of(starts, row_ids):
    return jnp.sum((starts[None, :] <= row_ids[:, None]).astype(jnp.int32), axis=1) - 1


def exact_dot(left, right):
    return jnp.dot(left, right, precision=lax.Precision.HIGHEST, preferred_element_type=jnp.float32)


def contract(left, right, left_dim, right_dim):
    return lax.dot_general(
        left, right, (((left_dim,), (right_dim,)), ((), ())), preferred_element_type=jnp.float32
    )


def on_device(
    features,
    branch_weight,
    branch_gain,
    branch_shift,
    trunk_weight,
    trunk_gain,
    trunk_shift,
    class_weight,
    class_bias,
    heights,
    logit_grad,
):
    rows_dev, width, channels = features.shape
    branch_ch = branch_weight.shape[2]
    classes = class_weight.shape[1]
    images = heights.shape[0]
    most_side = max(bin_sides)
    pix_count = lax.axis_size("pix")
    br_count = lax.axis_size("br")
    pix_at = lax.axis_index("pix")
    br_at = lax.axis_index("br")
    side = jnp.sum(
        jnp.where(
            jnp.arange(len(bin_sides), dtype=jnp.int32) == br_at, jnp.array(bin_sides, jnp.int32), 0
        )
    )
    starts = jnp.cumsum(heights) - heights
    row_ids = pix_at * rows_dev + jnp.arange(rows_dev, dtype=jnp.int32)
    image = image_of(starts, row_ids)
    owner = image[:, None] == jnp.arange(images, dtype=jnp.int32)[None, :]
    height = jnp.sum(jnp.where(owner, heights[None, :], 0), axis=1)
    place = row_ids - jnp.sum(jnp.where(owner, starts[None, :], 0), axis=1)
    bin_ids = jnp.arange(most_side, dtype=jnp.int32)
    in_use = bin_ids < side
    lower = bin_ids[None, :] * height[:, None] // side
    upper = ((bin_ids[None, :] + 1) * height[:, None] + side - 1) // side
    member = in_use[None, :] & (place[:, None] >= lower) & (place[:, None] < upper)
    row_hot = (
        (owner.T[:, None, :] & member.T[None, :, :])
        .reshape(images * most_side, rows_dev)
        .astype(jnp.float32)
    )
    image_low = bin_ids[None, :] * heights[:, None] // side
    image_up = ((bin_ids[None, :] + 1) * heights[:, None] + side - 1) // side
    col_ids = jnp.arange(width, dtype=jnp.int32)
    col_low = bin_ids * width // side
    col_up = ((bin_ids + 1) * width + side - 1) // side
    col_mask = (
        in_use[:, None]
        & (col_ids[None, :] >= col_low[:, None])
        & (col_ids[None, :] < col_up[:, None])
    ).astype(jnp.float32)
    valid = in_use[:, None] & in_use[None, :]
    counts = jnp.where(
        valid[None], (image_up - image_low)[:, :, None] * (col_up - col_low)[None, None, :], 1
    ).astype(jnp.float32)
    valid_f = valid.astype(jnp.float32)[None, :, :, None]
    numer = (2 * place + 1) * side - height
    ahead = numer >= 0
    first = jnp.where(ahead, numer // (2 * height), 0)
    frac = jnp.where(
        ahead,
        (numer - 2 * height * first).astype(jnp.float32) / (2 * height).astype(jnp.float32),
        0.0,
    )
    second = jnp.minimum(first + 1, side - 1)
    col_numer = (2 * col_ids + 1) * side - width
    col_ahead = col_numer >= 0
    col_first = jnp.where(col_ahead, col_numer // (2 * width), 0)
    col_frac = jnp.where(
        col_ahead, (col_numer - 2 * width * col_first).astype(jnp.float32) / (2.0 * width), 0.0
    )
    col_second = jnp.minimum(col_first + 1, side - 1)
    col_weight = (1.0 - col_frac)[:, None] * (bin_ids[None, :] == col_first[:, None]).astype(
        jnp.float32
    )
    col_weight = col_weight + col_frac[:, None] * (bin_ids[None, :] == col_second[:, None]).astype(
        jnp.float32
    )
    flat_features = features.reshape(rows_dev * width, channels)
    proj = jnp.dot(flat_features, branch_weight[0], preferred_element_type=jnp.float32).reshape(
        rows_dev, width, branch_ch
    )
    col_sum = jnp.einsum("jx,rxc->rjc", col_mask, proj, precision=lax.Precision.HIGHEST)
    pool_part = exact_dot(row_hot, col_sum.reshape(rows_dev, most_side * branch_ch))
    sums = lax.psum(pool_part, "pix").reshape(images, most_side, most_side, branch_ch)
    pooled = sums / counts[..., None]
    total_bins = (images * side * side).astype(jnp.float32)
    centre = jnp.sum(pooled * valid_f, axis=(0, 1, 2)) / total_bins
    centred = (pooled - centre) * valid_f
    b_inv = lax.rsqrt(jnp.sum(centred * centred, axis=(0, 1, 2)) / total_bins + norm_eps)
    b_hat = centred * b_inv
    normed = b_hat * branch_gain[0] + branch_shift[0]
    active = (activate(normed) * valid_f).reshape(images * most_side, most_side, branch_ch)
    row_mix = (1.0 - frac)[:, None, None] * active[image * most_side + first] + frac[
        :, None, None
    ] * active[image * most_side + second]
    upsampled = jnp.einsum(
        "xj,rjc->rxc", col_weight, row_mix, precision=lax.Precision.HIGHEST
    ).astype(jnp.bfloat16)
    slice_width = channels // br_count
    own_slice = lax.dynamic_slice_in_dim(features, br_at * slice_width, slice_width, 2)
    joined = jnp.concatenate([own_slice, upsampled], axis=2)
    in_width = joined.shape[2]
    padded = padded_2(joined, (("pix", 0),), 1)
    padded = jnp.pad(padded, ((0, 0), (1, 1), (0, 0)))
    pad_image = image_of(starts, pix_at * rows_dev - 1 + jnp.arange(rows_dev + 2, dtype=jnp.int32))

    def same_image(row_step):
        return (pad_image[1 + row_step : 1 + row_step + rows_dev] == image).astype(jnp.bfloat16)[
            :, None, None
        ]

    summed = jnp.zeros((rows_dev * width, branch_ch), jnp.float32)
    for row_step in (-1, 0, 1):
        band = padded[1 + row_step : 1 + row_step + rows_dev] * same_image(row_step)
        for col_step in (-1, 0, 1):
            window = band[:, 1 + col_step : 1 + col_step + width].reshape(-1, in_width)
            summed = summed + jnp.dot(
                window,
                trunk_weight[0, row_step + 1, col_step + 1],
                preferred_element_type=jnp.float32,
            )
    summed = summed.reshape(rows_dev, width, branch_ch)
    quarter = branch_ch // br_count
    total_pix = float(rows_dev * width * pix_count)
    share = lax.psum_scatter(summed, "br", scatter_dimension=2, tiled=True)
    gain_slice = lax.dynamic_slice_in_dim(trunk_gain, br_at * quarter, quarter, 0)
    shift_slice = lax.dynamic_slice_in_dim(trunk_shift, br_at * quarter, quarter, 0)
    weight_slice = lax.dynamic_slice_in_dim(class_weight, br_at * quarter, quarter, 0)
    first_sum = jnp.sum(share, axis=(0, 1))
    square_sum = jnp.sum(share * share, axis=(0, 1))
    first_sum, square_sum = lax.psum((first_sum, square_sum), "pix")
    t_mean = first_sum / total_pix
    t_inv = lax.rsqrt(square_sum / total_pix - t_mean * t_mean + norm_eps)
    t_hat = (share - t_mean) * t_inv
    t_norm = t_hat * gain_slice + shift_slice
    hidden = activate(t_norm).astype(jnp.bfloat16).reshape(-1, quarter)
    logit_terms = jnp.dot(hidden, weight_slice, preferred_element_type=jnp.float32).reshape(
        rows_dev, width, classes
    )
    logits = lax.psum_scatter(logit_terms, "br", scatter_dimension=0, tiled=True) + class_bias
    grad_all = lax.all_gather(logit_grad, "br", axis=0, tiled=True)
    grad_flat = grad_all.reshape(-1, classes)
    weight_part = contract(hidden, grad_flat, 0, 0)
    bias_part = jnp.sum(grad_flat.astype(jnp.float32), axis=0)
    d_hidden = contract(grad_flat, weight_slice, 1, 1).reshape(share.shape)
    d_norm = d_hidden * gelu_slope(t_norm)
    gain_part = jnp.sum(d_norm * t_hat, axis=(0, 1))
    shift_part = jnp.sum(d_norm, axis=(0, 1))
    weight_part, bias_part, gain_part, shift_part = lax.psum(
        (weight_part, bias_part, gain_part, shift_part), "pix"
    )
    d_share = (
        gain_slice * t_inv * (d_norm - shift_part / total_pix - t_hat * gain_part / total_pix)
    ).astype(jnp.bfloat16)
    d_summed = lax.all_gather(d_share, "br", axis=2, tiled=True)
    d_padded = padded_2(d_summed, (("pix", 0),), 1)
    d_padded = jnp.pad(d_padded, ((0, 0), (1, 1), (0, 0)))
    d_flat = d_summed.reshape(-1, branch_ch)
    d_joined = jnp.zeros((rows_dev * width, in_width), jnp.float32)
    tap_rows = []
    for row_step in (-1, 0, 1):
        band = padded[1 + row_step : 1 + row_step + rows_dev] * same_image(row_step)
        back_band = d_padded[1 - row_step : 1 - row_step + rows_dev] * same_image(-row_step)
        tap_cols = []
        for col_step in (-1, 0, 1):
            window = band[:, 1 + col_step : 1 + col_step + width].reshape(-1, in_width)
            tap_cols.append(contract(window, d_flat, 0, 0))
            source = back_band[:, 1 - col_step : 1 - col_step + width].reshape(-1, branch_ch)
            d_joined = d_joined + contract(
                source, trunk_weight[0, row_step + 1, col_step + 1], 1, 1
            )
        tap_rows.append(jnp.stack(tap_cols))
    weight_term = jnp.stack(tap_rows)[None]
    trunk_weight_grad = lax.psum_scatter(weight_term, "pix", scatter_dimension=3, tiled=True)
    d_joined = d_joined.reshape(rows_dev, width, in_width)
    d_own = d_joined[:, :, :slice_width]
    d_upsampled = d_joined[:, :, slice_width:]
    d_row_mix = jnp.einsum("xj,rxc->rjc", col_weight, d_upsampled, precision=lax.Precision.HIGHEST)
    mix_weight = (bin_ids[:, None] == first[None, :]).astype(jnp.float32) * (1.0 - frac)[None, :]
    mix_weight = (
        mix_weight + (bin_ids[:, None] == second[None, :]).astype(jnp.float32) * frac[None, :]
    )
    interp_hot = (owner.T.astype(jnp.float32)[:, None, :] * mix_weight[None, :, :]).reshape(
        images * most_side, rows_dev
    )
    d_bin_part = exact_dot(interp_hot, d_row_mix.reshape(rows_dev, most_side * branch_ch))
    d_active = lax.psum(d_bin_part, "pix").reshape(images, most_side, most_side, branch_ch)
    d_normed = d_active * valid_f * gelu_slope(normed)
    branch_gain_part = jnp.sum(d_normed * b_hat, axis=(0, 1, 2))
    branch_shift_part = jnp.sum(d_normed, axis=(0, 1, 2))
    d_pooled = (
        branch_gain[0]
        * b_inv
        * (d_normed - branch_shift_part / total_bins - b_hat * branch_gain_part / total_bins)
        * valid_f
    )
    d_sums = d_pooled / counts[..., None]
    d_col = exact_dot(row_hot.T, d_sums.reshape(images * most_side, most_side * branch_ch)).reshape(
        rows_dev, most_side, branch_ch
    )
    d_proj = jnp.einsum("jx,rjc->rxc", col_mask, d_col, precision=lax.Precision.HIGHEST).astype(
        jnp.bfloat16
    )
    d_proj_flat = d_proj.reshape(-1, branch_ch)
    branch_term = contract(flat_features, d_proj_flat, 0, 0)[None]
    branch_weight_grad = lax.psum_scatter(branch_term, "pix", scatter_dimension=1, tiled=True)
    feature_term = contract(d_proj_flat, branch_weight[0], 1, 1).reshape(rows_dev, width, channels)
    feature_grad = (
        lax.psum_scatter(
            feature_term.astype(jnp.bfloat16), "br", scatter_dimension=2, tiled=True
        ).astype(jnp.float32)
        + d_own
    )
    return (
        logits.astype(jnp.bfloat16),
        feature_grad,
        branch_weight_grad,
        branch_gain_part[None],
        branch_shift_part[None],
        trunk_weight_grad,
        gain_part,
        shift_part,
        weight_part,
        bias_part,
    )


def solution(mesh):
    in_specs = (
        P("pix", None, None),
        P("br", None, None),
        P("br", None),
        P("br", None),
        P("br", None, None, None, None),
        P(),
        P(),
        P(),
        P(),
        P(),
        P(("pix", "br"), None, None),
    )
    out_specs = (
        P(("pix", "br"), None, None),
        P("pix", None, "br"),
        P("br", "pix", None),
        P("br", None),
        P("br", None),
        P("br", None, None, "pix", None),
        P("br"),
        P("br"),
        P("br", None),
        P(),
    )
    return jax.shard_map(
        on_device, mesh=mesh, in_specs=in_specs, out_specs=out_specs, check_vma=False
    )
```

profile of v0, /device:TPU:23, one launch (start us, length us, event | category | flops | bytes accessed | tf_op | source)
XLA Modules:
  0.0 949.5 jit_solution(17049121852630974573)
XLA Ops:
  16.1 5.5 fusion.11
  34.8 2.7 constant_dynamic-slice_fusion
  38.2 66.1 %all-reduce.8.cloned.1.call-done = f32[96,3072]{1,0:T(8,128)} async-done(((f32[96,3072]{1,0:T(8,128)}), f32[96,3072]{1,0:T(8,128)}) %all-reduce.8.cloned.1.call-update) | async-done | bytes 1179664 | tf_op jit(solution)/shard_map/psum | solution.py:136
  104.3 2.9 multiply_reduce_fusion.2
  108.8 2.9 reshape.952
  111.7 3.5 fusion.22
  115.2 2.7 gather_fusion.1
  117.9 2.7 gather_fusion
  120.6 3.9 fusion.25
  126.8 3.6 collective-permute-start.1
  130.4 3.0 collective-permute-done.1
  133.4 3.1 select_maximum_fusion
  142.3 3.5 fusion.167
  145.9 5.8 fusion.58
  151.7 4.3 convolution_add_fusion.7
  166.8 3.8 convolution_add_fusion
  172.0 10.4 %all_gather.6 = bf16[24,64,150]{2,1,0:T(8,128)(2,1)S(1)} all-gather(bf16[6,64,150]{2,1,0:T(8,128)(2,1)S(1)} %copy-done.13), channel_id=1, replica_groups=mesh['pix'=8,'br'=4] {'br'}, dimensions={0}, use_global_device_ids=true | all-gather | bytes 576000 | tf_op jit(solution)/shard_map/all_gather | solution.py:193
  185.4 2.3 copy.59
  189.1 21.1 %reduce-scatter.6.cloned.1.call-done = f32[24,64,128]{2,1,0:T(8,128)} async-done(((f32[24,64,512]{2,1,0:T(8,128)}), f32[24,64,128]{2,1,0:T(8,128)}) %reduce-scatter.6.cloned.1.call-update) | async-done | bytes 786448 | tf_op jit(solution)/shard_map/reduce_scatter | solution.py:177
  211.5 11.9 %all-reduce.3 = (f32[128]{0:T(128)S(1)}, f32[128]{0:T(128)S(1)}) all-reduce(f32[128]{0:T(128)S(1)} %get-tuple-element.65, f32[128]{0:T(128)S(1)} %get-tuple-element.64), channel_id=1, replica_groups=mesh['pix'=8,'br'=4] {'pix'}, use_global_device_ids=true, to_apply=%region_15.16 | all-reduce | flops 256 | bytes 2048 | tf_op jit(solution)/shard_map/psum | solution.py:183
  224.2 2.9 fusion.158
  227.1 15.9 %all-reduce.2 = (f32[128]{0:T(128)S(1)}, f32[128]{0:T(128)S(1)}, f32[150]{0:T(256)}) all-reduce(f32[128]{0:T(128)S(1)} %get-tuple-element.63, f32[128]{0:T(128)S(1)} %get-tuple-element.62, f32[150]{0:T(256)S(1)} %convert_reduce_fusion), channel_id=1, replica_groups=mesh['pix'=8,'br'=4] {'pix'}, use_global_device_ids=true, to_apply=%region_20.21 | all-reduce | flops 406 | bytes 3248 | tf_op jit(solution)/shard_map/psum | solution.py:201
  243.0 2.3 multiply_convert_fusion
  245.5 29.3 %all-gather.2.cloned.1.call-done = bf16[24,64,512]{2,1,0:T(8,128)(2,1)} async-done(((bf16[24,64,128]{2,1,0:T(8,128)(2,1)}), bf16[24,64,512]{2,1,0:T(8,128)(2,1)}) %all-gather.2.cloned.1.call-update) | async-done | bytes 1572880 | tf_op jit(solution)/shard_map/all_gather | solution.py:207
  275.8 3.1 collective-permute-start.2
  281.1 2.7 convolution_bitcast_fusion.11
  289.7 4.4 fusion.53
  294.1 4.5 fusion.56
  299.7 4.5 fusion.44
  304.2 4.4 fusion.50
  310.7 4.9 fusion.38
  315.6 4.6 fusion.41
  320.2 4.6 fusion.47
  324.7 4.5 fusion.60
  329.2 21.9 %add_add_fusion = f32[1536,1024]{1,0:T(8,128)} fusion(f32[1536,1024]{1,0:T(8,128)} %fusion.38, f32[1536,1024]{1,0:T(8,128)} %fusion.41, f32[1536,1024]{1,0:T(8,128)} %fusion.44, f32[1536,1024]{1,0:T(8,128)} %fusion.47, f32[1536,1024]{1,0:T(8,128)} %fusion.50, f32[1536,1024]{1,0:T(8,128)} %fusion.53, f32[1536,1024]{1,0:T(8,128)} %fusion.60, ...), kind=kOutput, calls=%fused_computation.9 | convolution fusion | flops 1623195648 | bytes 59244544 | tf_op jit(solution)/shard_map/dot_general | solution.py:45
  351.1 3.6 fusion.5
  357.2 2.8 fusion.95
  360.0 79.8 %all-reduce.10.cloned.1.call-done = (f32[96,3072]{1,0:T(8,128)}, f32[128,150]{0,1:T(8,128)}) async-done(((f32[96,3072]{1,0:T(8,128)}, f32[128,150]{0,1:T(8,128)}), (f32[96,3072]{1,0:T(8,128)}, f32[128,150]{0,1:T(8,128)})) %all-reduce.10.cloned.1.call-update) | async-done | bytes 1256464 | tf_op jit(solution)/shard_map/psum | solution.py:239
  439.8 3.7 fusion.157
  443.7 2.5 multiply_divide_fusion
  449.4 8.2 convolution_bitcast_fusion
  457.7 6.9 convolution_convert_fusion
  464.8 4.5 convolution_bitcast_fusion.3
  488.9 7.0 maximum_bitcast_fusion
  498.3 64.6 %reduce-scatter.12.cloned.1.call-done = f32[1,256,512]{1,2,0:T(8,128)} async-done(((f32[1,2048,512]{1,2,0:T(8,128)}), f32[1,256,512]{1,2,0:T(8,128)}) %reduce-scatter.12.cloned.1.call-update) | async-done | bytes 524304 | tf_op jit(solution)/shard_map/reduce_scatter | solution.py:258
  565.0 58.1 %reduce-scatter.10.cloned.1.call-done = bf16[24,64,512]{2,1,0:T(8,128)(2,1)} async-done(((bf16[24,64,2048]{2,1,0:T(8,128)(2,1)}), bf16[24,64,512]{2,1,0:T(8,128)(2,1)}) %reduce-scatter.10.cloned.1.call-update) | async-done | bytes 1572880 | tf_op jit(solution)/shard_map/reduce_scatter | solution.py:261
  623.1 4.7 slice_add_fusion
  627.7 314.1 %reduce-scatter.14.cloned.1.call-done = f32[1,3,3,128,512]{4,3,2,1,0:T(8,128)} async-done(((f32[1,3,3,1024,512]{4,3,2,1,0:T(8,128)}), f32[1,3,3,128,512]{4,3,2,1,0:T(8,128)}) %reduce-scatter.14.cloned.1.call-update) | async-done | bytes 2359312 | tf_op jit(solution)/shard_map/reduce_scatter | solution.py:226
  (236 shorter events, 91.2 us)
Async XLA Ops:
  7.2 8.9 copy-start
  7.2 97.1 %all-reduce.8.cloned.1.call-start = ((), (), s32[]{:S(2)}) async-start(), calls=%async_computation.5 | async-start | bytes 2359296 | tf_op jit(solution)/shard_map/psum | solution.py:136
  13.8 7.7 copy-start.22
  13.9 7.7 copy-start.24
  15.2 22.4 %copy-start.20 = (s32[24]{0:T(128)}, s32[24]{0:T(128)S(1)}, u32[]{:S(2)}) copy-start(s32[24]{0:T(128)S(1)} %get-tuple-element.79) | copy-start | bytes 292
  21.6 4.6 copy-start.19
  24.6 185.6 %reduce-scatter.6.cloned.1.call-start = ((), (), s32[]{:S(2)}) async-start(), calls=%async_computation.6 | async-start | bytes 3932160 | tf_op jit(solution)/shard_map/reduce_scatter | solution.py:177
  26.2 94.4 %copy-start.26 = (f32[64]{0:T(128)}, f32[64]{0:T(128)S(1)}, u32[]{:S(2)}) copy-start(f32[64]{0:T(128)S(1)} %get-tuple-element.135) | copy-start | bytes 772
  26.2 94.4 %copy-start.28 = (f32[64]{0:T(128)}, f32[64]{0:T(128)S(1)}, u32[]{:S(2)}) copy-start(f32[64]{0:T(128)S(1)} %get-tuple-element.136) | copy-start | bytes 772
  104.3 4.5 copy-start.15
  107.3 4.4 copy-start.16
  120.6 3.9 copy-start.7
  124.6 5.8 collective-permute-start
  126.8 6.6 collective-permute-start.1
  137.4 2.9 copy-start.3
  137.4 4.9 copy-start.1
  145.8 5.8 copy-start.9
  145.9 10.1 %slice-start = ((s8[9437184]{0:T(1024)(128)(4,1)}), s8[4194304]{0:T(1024)(128)(4,1)S(1)}, s32[]{:S(2)}) async-start(s8[9437184]{0:T(1024)(128)(4,1)} %bitcast.266), calls=%async_computation.13 | async-start | bytes 8388608
  145.9 10.1 %slice-start.1 = ((s8[9437184]{0:T(1024)(128)(4,1)}), s8[4194304]{0:T(1024)(128)(4,1)S(1)}, s32[]{:S(2)}) async-start(s8[9437184]{0:T(1024)(128)(4,1)} %bitcast.266), calls=%async_computation.14 | async-start | bytes 8388608
  151.7 4.3 slice-start.2
  170.7 104.1 %all-gather.2.cloned.1.call-start = ((), (), s32[]{:S(2)}) async-start(), calls=%async_computation.8 | async-start | bytes 1966080 | tf_op jit(solution)/shard_map/all_gather | solution.py:207
  182.5 41.7 %copy-start.35 = (f32[128]{0:T(128)S(1)}, f32[128]{0:T(128)}, u32[]{:S(2)}) copy-start(f32[128]{0:T(128)} %dynamic_slice.14) | copy-start | bytes 1540
  187.7 57.7 %copy-start.21 = (s32[24]{0:T(128)S(1)}, s32[24]{0:T(128)}, u32[]{:S(2)}) copy-start(s32[24]{0:T(128)} %copy-done.20) | copy-start | bytes 292
  187.7 57.7 %copy-start.32 = (s32[24]{0:T(128)S(1)}, s32[24]{0:T(128)}, u32[]{:S(2)}) copy-start(s32[24]{0:T(128)} %get-tuple-element.78) | copy-start | bytes 292
  224.2 21.3 %copy-start.30 = (f32[128]{0:T(128)}, f32[128]{0:T(128)S(1)}, u32[]{:S(2)}) copy-start(f32[128]{0:T(128)S(1)} %get-tuple-element.82) | copy-start | bytes 1540
  243.0 2.5 copy-start.34
  243.0 2.5 copy-start.37
  245.4 194.5 %all-reduce.10.cloned.1.call-start = ((), (), s32[]{:S(2)}) async-start(), calls=%async_computation.12 | async-start | bytes 2514944 | tf_op jit(solution)/shard_map/psum | solution.py:239
  274.8 10.0 %copy-start.10 = (bf16[24,64,512]{2,1,0:T(8,128)(2,1)S(1)}, bf16[24,64,512]{2,1,0:T(8,128)(2,1)}, u32[]{:S(2)}) copy-start(bf16[24,64,512]{2,1,0:T(8,128)(2,1)} %all-gather.2.cloned.1.call-done) | copy-start | bytes 4718596
  275.8 8.0 collective-permute-start.2
  278.9 5.9 collective-permute-start.3
  285.9 3.5 slice-start.4
  286.3 3.3 slice-start.5
  329.2 21.9 %copy-start.27 = (f32[64]{0:T(128)S(1)}, f32[64]{0:T(128)}, u32[]{:S(2)}) copy-start(f32[64]{0:T(128)} %copy-done.26) | copy-start | bytes 772
  329.2 21.9 %copy-start.29 = (f32[64]{0:T(128)S(1)}, f32[64]{0:T(128)}, u32[]{:S(2)}) copy-start(f32[64]{0:T(128)} %copy-done.28) | copy-start | bytes 772
  351.1 6.1 copy-start.31
  351.1 6.1 copy-start.36
  357.0 139.0 %reduce-scatter.8.cloned.1.call-start = ((), (), s32[]{:S(2)}) async-start(), calls=%async_computation.7 | async-start | bytes 1966080 | tf_op jit(solution)/shard_map/reduce_scatter | solution.py:192
  360.0 203.0 %reduce-scatter.12.cloned.1.call-start = ((), (), s32[]{:S(2)}) async-start(), calls=%async_computation.10 | async-start | bytes 4718592 | tf_op jit(solution)/shard_map/reduce_scatter | solution.py:258
  443.6 3.1 copy-start.18
  443.6 3.0 copy-start.17
  443.7 3.0 copy-start.23
  443.7 3.0 copy-start.25
  457.6 165.4 %reduce-scatter.10.cloned.1.call-start = ((), (), s32[]{:S(2)}) async-start(), calls=%async_computation.9 | async-start | bytes 7864320 | tf_op jit(solution)/shard_map/reduce_scatter | solution.py:261
  464.5 477.3 %reduce-scatter.14.cloned.1.call-start = ((), (), s32[]{:S(2)}) async-start(), calls=%async_computation.11 | async-start | bytes 21233664 | tf_op jit(solution)/shard_map/reduce_scatter | solution.py:226
  464.8 4.5 copy-start.6
  464.8 4.5 copy-start.11
  565.0 376.8 %copy-start.14 = (f32[128,150]{0,1:T(8,128)S(1)}, f32[128,150]{0,1:T(8,128)}, u32[]{:S(2)}) copy-start(f32[128,150]{0,1:T(8,128)} %get-tuple-element.147) | copy-start | bytes 230404
  (8 other events, 12.4 us)
Sparse Core Ops, SparseCore 0:
  24.7 79.5 all-reduce.7
  170.8 39.3 reduce-scatter.5
  245.5 29.2 all-gather.1
  357.1 82.6 all-reduce.9
  442.9 27.2 reduce-scatter.7
  473.7 89.1 reduce-scatter.11
  565.6 57.3 reduce-scatter.9
  627.5 314.2 reduce-scatter.13
where the time goes:
time: 956 us; the launch traced here: 950 us
  waiting for transfers between devices  637 us (67%)
  matrix products  145 us (15%)
  other arithmetic  55.8 us (6%)
  local copies, waits for them, and re-layouts  44 us (5%)
  blocking collectives  38.2 us (4%)
  between operations  18 us (2%)
  starting transfers between devices  11.8 us (1%)
    reduce_scatter x1, waiting for transfers between devices, on_device(): lax.psum_scatter(weight_term, 'pix', scatter_dimension=3, tiled=True)  314 us
    dot_general x22, matrix products, contract(): lax.dot_general(left, right, (((left_dim,), (right_dim,)), ((), ())), pre...  97.2 us
    psum x1, waiting for transfers between devices, on_device(): lax.psum(d_bin_part, 'pix').reshape(images, most_side, most_side, branch_ch)  79.8 us
    psum x1, waiting for transfers between devices, on_device(): lax.psum(pool_part, 'pix').reshape(images, most_side, most_side, branch_ch)  66.1 us
    reduce_scatter x1, waiting for transfers between devices, on_device(): lax.psum_scatter(branch_term, 'pix', scatter_dimension=1, tiled=True)  64.6 us
    reduce_scatter x1, waiting for transfers between devices, on_device(): lax.psum_scatter(feature_term.astype(jnp.bfloat16), 'br', scatter_dimensi...  58.1 us
    all_gather x1, waiting for transfers between devices, on_device(): d_summed = lax.all_gather(d_share, 'br', axis=2, tiled=True)  29.3 us
    dot_general x9, matrix products, on_device(): jnp.dot(window, trunk_weight[0, row_step + 1, col_step + 1], preferred_el...  24.7 us
  transfers between devices with their start and end apart: 12, of which 9 were waited for; matrix products, arithmetic and copies ran while one was open for 9% of the time, Pallas kernels for 0%

commit v1 on v0

v1 whole, which is shorter than its diff:
```python
import functools

import jax
import jax.numpy as jnp
import numpy as np
from jax import lax
from jax.experimental import pallas as pl
from jax.experimental.pallas import tpu as pltpu
from jax.sharding import PartitionSpec as P

bin_sides = (1, 2, 3, 6)
norm_eps = 1e-05


def padded_2(cells, sides, width):
    for axis, dim in sides:
        count = lax.axis_size(axis)
        ends = count - 1
        head = lax.slice_in_dim(cells, 0, width, axis=dim)
        tail = lax.slice_in_dim(cells, cells.shape[dim] - width, cells.shape[dim], axis=dim)
        cells = jnp.concatenate(
            [
                lax.ppermute(tail, axis, [(i, (i + 1) % count) for i in range(ends)]),
                cells,
                lax.ppermute(head, axis, [((i + 1) % count, i) for i in range(ends)]),
            ],
            axis=dim,
        )
    return cells


def activate(value):
    return jax.nn.gelu(value, approximate=True)


def gelu_slope(value):
    unused, pull = jax.vjp(activate, value)
    return pull(jnp.ones_like(value))[0]


def image_of(starts, row_ids):
    return jnp.sum((starts[None, :] <= row_ids[:, None]).astype(jnp.int32), axis=1) - 1


def exact_dot(left, right):
    return jnp.dot(left, right, precision=lax.Precision.HIGHEST, preferred_element_type=jnp.float32)


def contract(left, right, left_dim, right_dim):
    return lax.dot_general(
        left, right, (((left_dim,), (right_dim,)), ((), ())), preferred_element_type=jnp.float32
    )


def row_columns(sides, width, most_side):
    out = np.zeros((len(sides), width, most_side), np.float32)
    for b, side in enumerate(sides):
        for x in range(width):
            numer = (2 * x + 1) * side - width
            first = numer // (2 * width) if numer >= 0 else 0
            frac = (numer - 2 * width * first) / (2.0 * width) if numer >= 0 else 0.0
            second = min(first + 1, side - 1)
            out[b, x, first] += 1.0 - frac
            out[b, x, second] += frac
    return out


def shifted_columns(sides, width, most_side):
    cols = row_columns(sides, width, most_side)
    out = np.zeros((len(sides), 3, width, most_side), np.float32)
    for at, step in enumerate((-1, 0, 1)):
        for x in range(width):
            if 0 <= x + step < width:
                out[:, at, x] = cols[:, x + step]
    return out


def column_bins(sides, width, most_side):
    out = np.zeros((len(sides), most_side, width), np.float32)
    for b, side in enumerate(sides):
        for j in range(side):
            out[b, j, j * width // side : ((j + 1) * width + side - 1) // side] = 1.0
    return out


def split_dot(left, right, **kw):
    high = left.astype(jnp.bfloat16)
    low = (left - high.astype(jnp.float32)).astype(jnp.bfloat16)
    return jnp.dot(high, right, preferred_element_type=jnp.float32) + jnp.dot(
        low, right, preferred_element_type=jnp.float32
    )


def on_device(
    features,
    branch_weight,
    branch_gain,
    branch_shift,
    trunk_weight,
    trunk_gain,
    trunk_shift,
    class_weight,
    class_bias,
    heights,
    logit_grad,
):
    rows_dev, width, channels = features.shape
    branch_ch = branch_weight.shape[2]
    classes = class_weight.shape[1]
    images = heights.shape[0]
    most_side = max(bin_sides)
    pix_count = lax.axis_size("pix")
    br_count = lax.axis_size("br")
    pix_at = lax.axis_index("pix")
    br_at = lax.axis_index("br")
    own_rows = rows_dev // br_count
    total_pix = float(rows_dev * width * pix_count)
    slice_width = channels // br_count
    bf16 = jnp.bfloat16
    side = jnp.sum(jnp.where(jnp.arange(len(bin_sides)) == br_at, jnp.array(bin_sides, jnp.int32), 0))
    starts = jnp.cumsum(heights) - heights
    bin_ids = jnp.arange(most_side, dtype=jnp.int32)
    in_use = bin_ids < side
    ext_ids = pix_at * rows_dev - 1 + jnp.arange(rows_dev + 2, dtype=jnp.int32)
    on_canvas = (ext_ids >= 0) & (ext_ids < rows_dev * pix_count)
    ext_image = jnp.where(on_canvas, image_of(starts, ext_ids), -1)
    owner = ext_image[:, None] == jnp.arange(images, dtype=jnp.int32)[None, :]
    height = jnp.maximum(jnp.sum(jnp.where(owner, heights[None, :], 0), axis=1), 1)
    place = ext_ids - jnp.sum(jnp.where(owner, starts[None, :], 0), axis=1)
    lower = bin_ids[None, :] * height[:, None] // side
    upper = ((bin_ids[None, :] + 1) * height[:, None] + side - 1) // side
    member = in_use[None, :] & (place[:, None] >= lower) & (place[:, None] < upper)
    row_hot = (
        (owner.T[:, None, :] & member.T[None, :, :])
        .reshape(images * most_side, rows_dev + 2)[:, 1:-1]
        .astype(jnp.float32)
    )
    numer = (2 * place + 1) * side - height
    ahead = numer >= 0
    first = jnp.where(ahead, numer // (2 * height), 0)
    frac = jnp.where(
        ahead,
        (numer - 2 * height * first).astype(jnp.float32) / (2 * height).astype(jnp.float32),
        0.0,
    )
    second = jnp.minimum(first + 1, side - 1)
    mix = (bin_ids[:, None] == first[None, :]).astype(jnp.float32) * (1.0 - frac)[None, :]
    mix = mix + (bin_ids[:, None] == second[None, :]).astype(jnp.float32) * frac[None, :]
    interp = (owner.T.astype(jnp.float32)[:, None, :] * mix[None]).reshape(
        images * most_side, rows_dev + 2
    )
    image_low = bin_ids[None, :] * heights[:, None] // side
    image_up = ((bin_ids[None, :] + 1) * heights[:, None] + side - 1) // side
    col_low = bin_ids * width // side
    col_up = ((bin_ids + 1) * width + side - 1) // side
    valid = in_use[:, None] & in_use[None, :]
    counts = jnp.where(
        valid[None], (image_up - image_low)[:, :, None] * (col_up - col_low)[None, None, :], 1
    ).astype(jnp.float32)
    valid_f = valid.astype(jnp.float32)[None, :, :, None]
    all_cols = jnp.asarray(shifted_columns(bin_sides, width, most_side))
    all_bins = jnp.asarray(column_bins(bin_sides, width, most_side), bf16)
    own_bins = lax.dynamic_index_in_dim(all_bins, br_at, 0, False)

    col_feat = jnp.einsum("jx,rxc->jrc", own_bins, features, preferred_element_type=jnp.float32)
    col_proj = split_dot(col_feat.reshape(-1, channels), branch_weight[0])
    col_proj = col_proj.reshape(most_side, rows_dev, branch_ch)
    pool_part = jnp.einsum("nr,jrc->njc", row_hot, col_proj, precision=lax.Precision.HIGHEST)
    sums = lax.psum(pool_part, "pix").reshape(images, most_side, most_side, branch_ch)
    pooled = sums / counts[..., None]
    total_bins = (images * side * side).astype(jnp.float32)
    centre = jnp.sum(pooled * valid_f, axis=(0, 1, 2)) / total_bins
    centred = (pooled - centre) * valid_f
    b_inv = lax.rsqrt(jnp.sum(centred * centred, axis=(0, 1, 2)) / total_bins + norm_eps)
    b_hat = centred * b_inv
    normed = b_hat * branch_gain[0] + branch_shift[0]
    active = (activate(normed) * valid_f).reshape(images * most_side, most_side, branch_ch)
    row_mix = jnp.einsum("nr,njc->rjc", interp, active, precision=lax.Precision.HIGHEST).astype(bf16)

    def keep(step):
        return (ext_image[1 + step : 1 + step + rows_dev] == ext_image[1:-1]).astype(bf16)

    own_slice = lax.dynamic_slice_in_dim(features, br_at * slice_width, slice_width, 2)
    feat_ext = padded_2(own_slice, (("pix", 0),), 1)
    feat_pad = jnp.pad(feat_ext, ((0, 0), (1, 1), (0, 0)))
    feat_weight = trunk_weight[0, :, :, :slice_width]
    up_weight = trunk_weight[0, :, :, slice_width:]
    feat_sum = jnp.zeros((rows_dev * width, branch_ch), jnp.float32)
    up_sum = [jnp.zeros((rows_dev * most_side, branch_ch), jnp.float32) for _ in range(3)]
    for at in range(3):
        band = feat_pad[at : at + rows_dev] * keep(at - 1)[:, None, None]
        up_band = (row_mix[at : at + rows_dev] * keep(at - 1)[:, None, None]).reshape(-1, branch_ch)
        for to in range(3):
            window = band[:, to : to + width].reshape(-1, slice_width)
            feat_sum = feat_sum + jnp.dot(
                window, feat_weight[at, to], preferred_element_type=jnp.float32
            )
            up_sum[to] = up_sum[to] + jnp.dot(
                up_band, up_weight[at, to], preferred_element_type=jnp.float32
            )
    pre = lax.psum_scatter(
        feat_sum.astype(bf16).reshape(rows_dev, width, branch_ch), "br", scatter_dimension=0, tiled=True
    ).astype(jnp.float32)
    up_all = jnp.stack(up_sum).reshape(3, br_count, own_rows, most_side, branch_ch).astype(bf16)
    up_all = lax.all_to_all(up_all, "br", 1, 0, tiled=False)
    pre = pre + jnp.einsum(
        "btxj,btrjc->rxc", all_cols.astype(bf16), up_all, preferred_element_type=jnp.float32
    )

    both = ("pix", "br")
    first_sum, square_sum = lax.psum((jnp.sum(pre, (0, 1)), jnp.sum(pre * pre, (0, 1))), both)
    t_mean = first_sum / total_pix
    t_inv = lax.rsqrt(square_sum / total_pix - t_mean * t_mean + norm_eps)
    t_hat = (pre - t_mean) * t_inv
    t_norm = t_hat * trunk_gain + trunk_shift
    hidden = activate(t_norm).astype(bf16).reshape(-1, branch_ch)
    logits = jnp.dot(hidden, class_weight, preferred_element_type=jnp.float32) + class_bias
    logits = logits.reshape(own_rows, width, classes).astype(bf16)
    grad_flat = logit_grad.reshape(-1, classes)
    weight_part = contract(hidden, grad_flat, 0, 0)
    bias_part = jnp.sum(grad_flat.astype(jnp.float32), axis=0)
    d_norm = contract(grad_flat, class_weight, 1, 1).reshape(pre.shape) * gelu_slope(t_norm)
    gain_part, shift_part, bias_part = lax.psum(
        (jnp.sum(d_norm * t_hat, (0, 1)), jnp.sum(d_norm, (0, 1)), bias_part), both
    )
    weight_part = lax.psum(lax.psum_scatter(weight_part, "br", scatter_dimension=0, tiled=True), "pix")
    d_pre = (
        trunk_gain * t_inv * (d_norm - shift_part / total_pix - t_hat * gain_part / total_pix)
    ).astype(bf16)

    d_cols = jnp.einsum(
        "btxj,rxc->btrjc", all_cols.astype(bf16), d_pre, preferred_element_type=jnp.float32
    ).astype(bf16)
    d_cols = lax.all_to_all(d_cols, "br", 0, 2, tiled=True)[0]
    d_mix = jnp.zeros((rows_dev + 2, most_side, branch_ch), jnp.float32)
    up_taps = []
    for at in range(3):
        part = jnp.zeros((rows_dev * most_side, branch_ch), jnp.float32)
        kept = d_cols * keep(at - 1)[None, :, None, None]
        up_band = row_mix[at : at + rows_dev].reshape(-1, branch_ch)
        for to in range(3):
            part = part + contract(kept[to].reshape(-1, branch_ch), up_weight[at, to], 1, 1)
            up_taps.append(contract(up_band, kept[to].reshape(-1, branch_ch), 0, 0))
        d_mix = d_mix.at[at : at + rows_dev].add(part.reshape(rows_dev, most_side, branch_ch))
    d_bin_part = jnp.einsum("nr,rjc->njc", interp, d_mix, precision=lax.Precision.HIGHEST)
    d_active = lax.psum(d_bin_part, "pix").reshape(images, most_side, most_side, branch_ch)
    d_normed = d_active * valid_f * gelu_slope(normed)
    branch_gain_part = jnp.sum(d_normed * b_hat, axis=(0, 1, 2))
    branch_shift_part = jnp.sum(d_normed, axis=(0, 1, 2))
    d_pooled = (
        branch_gain[0]
        * b_inv
        * (d_normed - branch_shift_part / total_bins - b_hat * branch_gain_part / total_bins)
        * valid_f
    )
    d_sums = (d_pooled / counts[..., None]).reshape(images * most_side, most_side, branch_ch)

    d_all = lax.all_gather(d_pre, "br", axis=0, tiled=True)
    d_pad = jnp.pad(padded_2(d_all, (("pix", 0),), 1), ((0, 0), (1, 1), (0, 0)))
    d_flat = d_all.reshape(-1, branch_ch)
    d_own = jnp.zeros((rows_dev * width, slice_width), jnp.float32)
    feat_taps = []
    for at in range(3):
        band = feat_pad[at : at + rows_dev] * keep(at - 1)[:, None, None]
        back = d_pad[2 - at : 2 - at + rows_dev] * keep(1 - at)[:, None, None]
        for to in range(3):
            window = band[:, to : to + width].reshape(-1, slice_width)
            feat_taps.append(contract(window, d_flat, 0, 0))
            source = back[:, 2 - to : 2 - to + width].reshape(-1, branch_ch)
            d_own = d_own + contract(source, feat_weight[at, to], 1, 1)
    taps = jnp.concatenate([jnp.stack(feat_taps), jnp.stack(up_taps)], axis=1).astype(bf16)
    trunk_weight_grad = lax.psum_scatter(taps, "pix", scatter_dimension=1, tiled=True)
    trunk_weight_grad = trunk_weight_grad.astype(jnp.float32).reshape(1, 3, 3, -1, branch_ch)

    d_col = jnp.einsum("nr,njc->jrc", row_hot, d_sums, precision=lax.Precision.HIGHEST).astype(bf16)
    spread = contract(d_col.reshape(-1, branch_ch), branch_weight[0], 1, 1).astype(bf16)
    spread = spread.reshape(1, most_side, rows_dev, br_count, slice_width)
    spread = lax.all_to_all(spread, "br", 3, 0, tiled=False)[:, 0]
    feature_grad = jnp.einsum(
        "bjx,bjrc->rxc", all_bins, spread, preferred_element_type=jnp.float32
    ) + d_own.reshape(rows_dev, width, slice_width)
    branch_term = contract(col_feat.astype(bf16).reshape(-1, channels), d_col.reshape(-1, branch_ch), 0, 0)
    branch_weight_grad = lax.psum_scatter(branch_term, "pix", scatter_dimension=0, tiled=True)[None]
    start = br_at * (branch_ch // br_count)
    return (
        logits,
        feature_grad,
        branch_weight_grad,
        branch_gain_part[None],
        branch_shift_part[None],
        trunk_weight_grad,
        lax.dynamic_slice_in_dim(gain_part, start, branch_ch // br_count, 0),
        lax.dynamic_slice_in_dim(shift_part, start, branch_ch // br_count, 0),
        weight_part,
        bias_part,
    )


MESH = pl.DeviceIdType.MESH
HIGH = lax.Precision.HIGHEST
F32 = jnp.float32
BF16 = jnp.bfloat16


def mod2(value, by):
    return lax.bitwise_and(value, jnp.full_like(value, by - 1))


def div2(value, by):
    return lax.shift_right_logical(value, jnp.full_like(value, by.bit_length() - 1))


def dot(left, right):
    return jnp.dot(left, right, preferred_element_type=F32)


def dot_nt(left, right):
    return lax.dot_general(left, right, (((1,), (1,)), ((), ())), preferred_element_type=F32)


def dot_tn(left, right):
    return lax.dot_general(left, right, (((0,), (0,)), ((), ())), preferred_element_type=F32)


def gelu_parts(value):
    inner = 0.7978845608 * (value + 0.044715 * value * value * value)
    tanh = jnp.tanh(inner)
    half = 0.5 * (1.0 + tanh)
    slope = half + 0.5 * value * (1.0 - tanh * tanh) * (
        0.7978845608 * (1.0 + 0.134145 * value * value)
    )
    return value * half, slope


class Shape:
    def __init__(self, features, branch_weight, class_weight, heights, pix, br):
        self.rows, self.width, self.channels = features.shape
        self.ch = branch_weight.shape[2]
        self.classes = class_weight.shape[1]
        self.images = heights.shape[0]
        self.pix, self.br = pix, br
        self.side = max(bin_sides)
        self.bins = self.side * self.images
        self.own = self.rows // br
        self.px = self.rows * self.width
        self.own_px = self.own * self.width
        self.all_rows = self.rows * pix


def fused_kernel(
    d,
    feat_hbm, bw_hbm, tw_hbm, x_hbm, xt_hbm, pool_hbm, spread_hbm,
    bgain, bshift, tgain, tshift, cweight_t, cbias, lgrad, heights,
    logits_out, fg_hbm, bwg_out, twg_hbm, cwg_out, small_out,
    fext, shifted, fgrp, wb, twf, twu, xc, xt, pool8, spread8,
    fc_hi, zsend, zrecv, fcrecv, pfsend, pfrecv, hidden,
    hot_all, mix_all, mix_t, hot_own, mrow, mrow2, mgrp,
    bhat, bnorm, binv, rmsend, rmrecv, actsend, actrecv, hsend, hrecv,
    st1, st2, st3, st4, sr1, sr2, sr3, sr4, tot,
    cwp, lgp, cwsend, cwr1, cw2, cwr2, cw3, cwr3,
    dpext, dpext2, drecv, drsend, drrecv, dwrecv, dssend, dsrecv, smsend, smrecv, ds_all,
    fp_all, fp_t, esend, erecv, fg, keep, sendx, recvz, upsend, uprecv, eye,
    load_sem, out_sem, twg_sem, halo_sem, z_sem, fc_sem, pf_sem, rm_sem, act_sem, h_sem,
    st_sem1, st_sem2, st_sem3, st_sem4, cw_sem1, cw_sem2, cw_sem3,
    dp_sem, dphalo_sem, dp2_sem, dphalo2_sem, fp_sem, dr_sem, dw_sem, ds_sem, sm_sem, e_sem, zz_sem, a_sem, up_sem,
):
    W, C, J, NB, P, B = d.width, d.ch, d.side, d.bins, d.pix, d.br
    PX, OPX, R, Q = d.px, d.own_px, d.rows, d.own
    HJ = J // 2
    lhs_rows = 8 * B * J
    pre = fg.at[pl.ds(3 * lhs_rows, OPX)]
    dnorm = fg.at[pl.ds(3 * lhs_rows + OPX, OPX)]
    p = lax.axis_index("pix")
    b = lax.axis_index("br")
    x_at = lax.rem(p, 2)
    z_at = lax.div(p, 2)
    x_peer = p + 1 - 2 * x_at
    core_peer = b + 1 - 2 * lax.rem(b, 2)
    y_peer = lax.rem(b + 2, B)
    side = jnp.where(b == 0, 1, jnp.where(b == 1, 2, jnp.where(b == 2, 3, 6)))
    side_f = side.astype(F32)

    def remote(src, dst, sem, at, axis, peer):
        return pltpu.make_async_remote_copy(
            src_ref=src, dst_ref=dst, send_sem=sem.at[0, at], recv_sem=sem.at[1, at],
            device_id={axis: peer}, device_id_type=MESH,
        )

    def exchange(axis, sem, src_of, dst_of):
        count, me = (P, p) if axis == "pix" else (B, b)
        copies = []
        for step in range(1, count):
            peer = lax.rem(me + step, count)
            copy = remote(src_of(peer), dst_of(me), sem, step - 1, axis, peer)
            copy.start()
            copies.append(copy)
        return copies

    def arrive(copies):
        for copy in copies:
            copy.wait_recv()

    pending = []

    own_lanes = pl.ds(pl.multiple_of(b * C, C), C)
    groups = R // 8
    gpx = 8 * W
    loads = {}

    def load(name, at, src, dst):
        loads[name] = pltpu.make_async_copy(src, dst, load_sem.at[at])
        loads[name].start()

    load("pool", 0, pool_hbm.at[b], pool8)
    for g in range(groups):
        load(f"feat{g}", 1 + g, feat_hbm.at[pl.ds(g * gpx, gpx)], fgrp.at[g])
    load("wb", 4, bw_hbm, wb)

    barrier = pltpu.get_barrier_semaphore()
    for step in range(1, P):
        pl.semaphore_signal(barrier, inc=1, device_id={"pix": lax.rem(p + step, P)}, device_id_type=MESH)
    for step in range(1, B):
        pl.semaphore_signal(barrier, inc=1, device_id={"br": lax.rem(b + step, B)}, device_id_type=MESH)

    for step in range(1, B):
        for to in (p + 1, p + P - 1, p + 2, p + P - 2):
            pl.semaphore_signal(
                barrier, inc=1, device_id={"pix": lax.rem(to, P), "br": lax.rem(b + step, B)},
                device_id_type=MESH,
            )

    tall = [heights[g] for g in range(d.images)]
    starts = [jnp.int32(0)]
    for g in range(d.images - 1):
        starts.append(starts[-1] + tall[g])

    def row_info(t):
        image = jnp.full(t.shape, -1, jnp.int32)
        height = jnp.ones(t.shape, jnp.int32)
        start = jnp.zeros(t.shape, jnp.int32)
        for g in range(d.images):
            reached = t >= starts[g]
            image = jnp.where(reached, g, image)
            height = jnp.where(reached, tall[g], height)
            start = jnp.where(reached, starts[g], start)
        image = jnp.where(t >= d.all_rows, -2, image)
        return image, height.astype(F32), (t - start).astype(F32)

    def bin_index(shape, axis):
        n = lax.broadcasted_iota(jnp.int32, shape, axis)
        return mod2(n, d.images), div2(n, d.images)

    def floor_div(a, by):
        return jnp.floor((a + 0.5) / by)

    def row_hot(t, g, i):
        image, height, place = row_info(t)
        i_f = i.astype(F32)
        lower = floor_div(i_f * height, side_f)
        upper = floor_div((i_f + 1.0) * height + (side_f - 1.0), side_f)
        inside = (image == g) & (i < side) & (place >= lower) & (place < upper)
        return jnp.where(inside, 1.0, 0.0)

    def row_mix(t, g, i, image_at=None):
        image, height, place = row_info(t)
        twice = 2.0 * height
        numer = (2.0 * place + 1.0) * side_f - height
        first = jnp.where(numer >= 0.0, floor_div(numer, twice), 0.0)
        frac = jnp.where(numer >= 0.0, (numer - twice * first) / twice, 0.0)
        second = jnp.minimum(first + 1.0, side_f - 1.0)
        i_f = i.astype(F32)
        value = jnp.where(i_f == first, 1.0 - frac, 0.0) + jnp.where(i_f == second, frac, 0.0)
        value = jnp.where(image == g, value, 0.0)
        if image_at is not None:
            value = jnp.where(image == image_at, value, 0.0)
        return value

    def halo_rows(shape, axis, first):
        n = lax.broadcasted_iota(jnp.int32, shape, axis)
        k, owner, dev = mod2(n, 8), mod2(div2(n, 8), B), div2(n, 8 * B)
        return first + dev * R + owner * Q + k, k

    g_col, i_col = bin_index((NB, 1), 0)
    g_row, i_row = bin_index((1, NB), 1)
    t_row = lax.broadcasted_iota(jnp.int32, (1, d.all_rows), 1)
    hot_all[...] = row_hot(t_row, g_col, i_col)
    t_own = lax.broadcasted_iota(jnp.int32, (R, 1), 0) + p * R
    hot_own[...] = row_hot(t_own, g_row, i_row)
    t_halo, _ = halo_rows((8 * B * P, 1), 0, -1)
    mix_all[...] = row_mix(t_halo, g_row, i_row)
    t_halo, _ = halo_rows((1, 8 * B * P), 1, -1)
    mix_t[...] = row_mix(t_halo, g_col, i_col)
    t_own = lax.broadcasted_iota(jnp.int32, (32, 128), 0) + p * R
    here = row_info(t_own)[0]
    t_peer = lax.broadcasted_iota(jnp.int32, (32, 128), 0) + x_peer * R
    here_peer = row_info(t_peer)[0]
    t_grp, k_grp = halo_rows((8 * B, 128), 0, p * R)
    here_grp = row_info(t_grp)[0]
    for at, step in enumerate((-1, 1)):
        mrow2[at] = jnp.where(row_info(t_peer + step)[0] == here_peer, 1.0, 0.0)
        mrow[at] = jnp.where(row_info(t_own + step)[0] == here, 1.0, 0.0)
        mgrp[at] = jnp.where((row_info(t_grp + step)[0] == here_grp) & (k_grp < Q), 1.0, 0.0)

    tall_col = jnp.ones((NB, 1), F32)
    for g in range(d.images):
        tall_col = jnp.where(g_col == g, tall[g].astype(F32), tall_col)
    i_f = i_col.astype(F32)
    row_count = floor_div((i_f + 1.0) * tall_col + (side_f - 1.0), side_f) - floor_div(
        i_f * tall_col, side_f
    )
    lane = lax.broadcasted_iota(jnp.int32, (1, HJ * 128), 1)
    j_lane = div2(lane, 128) + jnp.where(mod2(lane, 128) >= 64, HJ, 0)
    j_f = j_lane.astype(F32)
    col_count = floor_div((j_f + 1.0) * W + (side_f - 1.0), side_f) - floor_div(j_f * W, side_f)
    valid = (i_col < side) & (j_lane < side)
    valid_f = jnp.where(valid, 1.0, 0.0)
    count = jnp.where(valid, row_count * col_count, 1.0)
    total_bins = side_f * side_f * float(d.images)

    square = lax.broadcasted_iota(jnp.int32, (C, C), 0) == lax.broadcasted_iota(jnp.int32, (C, C), 1)
    eye[...] = jnp.where(square, 1.0, 0.0).astype(BF16)

    def turned(value):
        n = value.shape[1]
        return dot_nt(eye[0:n, 0:n], value).astype(BF16)

    def low(shape):
        return lax.broadcasted_iota(jnp.int32, shape, 1) < 64

    def swap(value):
        return pltpu.roll(value, 64, 1)

    def pack(left, right, odd):
        if odd:
            return jnp.where(low(left.shape), swap(left), right)
        return jnp.where(low(left.shape), left, swap(right))

    def unpack(even, odd):
        return (
            jnp.where(low(even.shape), even, swap(odd)),
            jnp.where(low(even.shape), swap(even), odd),
        )

    def both_halves(row):
        return row + swap(row)

    def over_bins(value):
        row = jnp.sum(value, axis=0, keepdims=True)
        return both_halves(row[:, :128] + row[:, 128:256] + row[:, 256:384])

    def thrice(row):
        return jnp.concatenate([row] * HJ, axis=1)

    def own_channels(ref):
        block = ref[:, pl.ds(pl.multiple_of(lax.div(p, 2) * 128, 128), 128)]
        other = swap(block)
        is_low = low(block.shape)
        even = jnp.where(is_low, block, other)
        odd = jnp.where(is_low, other, block)
        return jnp.where(x_at == 0, even, odd)

    loads["pool"].wait()
    col_parts = []
    for g in range(groups):
        loads[f"feat{g}"].wait()
        col_parts.append(dot(pool8[...], fgrp[g]))
    load("own", 5, feat_hbm.at[:, own_lanes], fext.at[pl.ds(W, PX)])
    for dy in range(3):
        for dx in range(3):
            load(f"twf{dy * 3 + dx}", 9 + dy * 3 + dx, tw_hbm.at[dy * 3 + dx, pl.ds(0, C)], twf.at[dx * 3 + 2 - dy])
            load(f"twu{dy * 3 + dx}", 18 + dy * 3 + dx, tw_hbm.at[dy * 3 + dx, pl.ds(C, C)], twu.at[dx * 3 + dy])
    load("x", 6, x_hbm, xc)
    load("xt", 7, xt_hbm, xt)
    load("spread", 8, spread_hbm, spread8)
    col_feat = jnp.concatenate(col_parts, axis=0)
    high = col_feat.astype(BF16)
    fc_hi[...] = high
    rest = (col_feat - high.astype(F32)).astype(BF16)
    loads["wb"].wait()
    rows_c = groups * J * 8
    proj2 = dot(jnp.concatenate([high, rest], axis=0), wb[...])
    proj = proj2[:rows_c] + proj2[rows_c:]
    for k in range(P // 2):
        block = proj[:, 128 * k : 128 * (k + 1)]

        def rows_of(j):
            return jnp.concatenate(
                [block[(g * J + j) * 8 : (g * J + j) * 8 + 8] for g in range(groups)], axis=0
            )

        for jj in range(HJ):
            left, right = rows_of(jj), rows_of(jj + HJ)
            for odd in range(2):
                zsend[2 * k + odd, :, 128 * jj : 128 * (jj + 1)] = pack(left, right, odd)

    pl.semaphore_wait(barrier, P - 1 + 5 * (B - 1))
    halo_down = remote(
        feat_hbm.at[pl.ds(PX - W, W), own_lanes], fext.at[pl.ds(0, W)], halo_sem, 0, "pix",
        lax.rem(p + 1, P),
    )
    halo_up = remote(
        feat_hbm.at[pl.ds(0, W), own_lanes], fext.at[pl.ds(W + PX, W)], halo_sem, 1, "pix",
        lax.rem(p + P - 1, P),
    )

    @pl.when(p < P - 1)
    def _():
        halo_down.start()

    @pl.when(p > 0)
    def _():
        halo_up.start()

    def peer_features(half):
        return remote(
            feat_hbm.at[:, pl.ds(pl.multiple_of(b * C + half * (C // 2) + (1 - x_at) * 128, 128), 128)],
            upsend.at[pl.ds(half * PX, PX)], fp_sem, half, "pix", x_peer,
        )

    fp_copies = [peer_features(0), peer_features(1)]
    def z_rows(at):
        return pl.ds(pl.multiple_of(at * R, 8), R)

    z_copies = exchange("pix", z_sem, lambda q: zsend.at[q], lambda me: zrecv.at[z_rows(me)])
    zrecv[z_rows(p), :] = zsend[p]
    pending.extend(z_copies)
    fp_copies[0].start()
    cshare = d.channels // P

    def fc_lanes(at):
        return pl.ds(pl.multiple_of(at * cshare, cshare), cshare)

    def shift_rows(source, masks, lanes_of):
        def step(r, carry):
            at = pl.multiple_of(r * W, W)
            for e in range(3):
                rows = source[pl.ds(pl.multiple_of((r + e) * W, W), W), :]
                if e != 1:
                    mask = masks[e // 2, pl.ds(r, 1), :]
                    mask = jnp.concatenate([mask] * (C // 128), axis=1)
                    rows = rows * jnp.broadcast_to(mask, rows.shape).astype(BF16)
                shifted[pl.ds(at, W), lanes_of(e)] = rows
            return carry

        lax.fori_loop(0, R, step, 0)

    def backward_lanes(e):
        return slice(e * C, (e + 1) * C)

    def forward_lanes(e):
        return backward_lanes(2 - e)

    def shift_columns(value, step):
        rows = value.shape[0]
        column = mod2(lax.broadcasted_iota(jnp.int32, value.shape, 0), W)
        if step == 1:
            return jnp.where(column == W - 1, 0.0, pltpu.roll(value, rows - 1, 0))
        return jnp.where(column == 0, 0.0, pltpu.roll(value, 1, 0))

    @pl.when(p == 0)
    def _():
        fext[pl.ds(0, W), :] = jnp.zeros((W, C), BF16)

    @pl.when(p == P - 1)
    def _():
        fext[pl.ds(W + PX, W), :] = jnp.zeros((W, C), BF16)

    @pl.when(p > 0)
    def _():
        halo_down.wait_recv()

    @pl.when(p < P - 1)
    def _():
        halo_up.wait_recv()

    loads["own"].wait()
    shift_rows(fext, mrow, forward_lanes)
    for tap in range(9):
        loads[f"twf{tap}"].wait()

    def conv_chunk(at, sign):
        rows = shifted[pl.ds(pl.multiple_of(at * OPX, W), OPX), :]
        total = None
        for dx in range(3):
            part = dot(rows, twf[3 * dx : 3 * dx + 3].reshape(3 * C, C))
            if dx != 1:
                part = shift_columns(part, sign * (dx - 1))
            total = part if total is None else total + part
        return total

    def pf_rows(at):
        return pl.ds(pl.multiple_of(at * OPX, OPX), OPX)

    def own_conv(at):
        return conv_chunk(at, 1)

    def pf_copy(step):
        return remote(pfsend.at[step], pfrecv.at[step], pf_sem, step, "br", core_peer)

    pf_copies = [pf_copy(0), pf_copy(1), remote(pfsend.at[2], pfrecv.at[2], pf_sem, 2, "br", y_peer)]
    pfsend[1] = own_conv(lax.rem(core_peer + 2, B)).astype(BF16)
    pf_copies[1].start()
    pre[...] = own_conv(y_peer)
    pf_copies[1].wait_recv()
    pfsend[2] = (pre[...] + pfrecv[1].astype(F32)).astype(BF16)
    pf_copies[2].start()

    cwp[...] = jnp.zeros_like(cwp)
    cwp[0 : d.classes, :] = cweight_t[...]
    lgp[...] = jnp.zeros_like(lgp)
    lgp[:, 0 : d.classes] = lgrad[...]
    dnorm[...] = dot(lgp[...], cwp[...])

    arrive(z_copies)
    sums = jnp.dot(hot_all[...], zrecv[...], precision=HIGH, preferred_element_type=F32)
    pooled = jnp.where(valid, sums / count, 0.0)
    centre = over_bins(pooled) / total_bins
    centred = (pooled - thrice(centre)) * valid_f
    spread = over_bins(centred * centred) / total_bins
    inv = lax.rsqrt(spread + norm_eps)
    hat = centred * thrice(inv)
    normed = hat * thrice(own_channels(bgain)) + thrice(own_channels(bshift))
    active = gelu_parts(normed)[0] * valid_f
    bhat[...] = hat
    bnorm[...] = normed
    binv[...] = jnp.broadcast_to(inv, (8, 128))
    rmsend[...] = jnp.dot(mix_all[...], active, precision=HIGH, preferred_element_type=F32).astype(BF16)

    def rm_rows(at):
        return pl.ds(pl.multiple_of(at * 8 * B, 8 * B), 8 * B)

    rm_copies = exchange("pix", rm_sem, lambda q: rmsend.at[rm_rows(q)], lambda me: rmrecv.at[rm_rows(me)])
    rmrecv[rm_rows(p), :] = rmsend[rm_rows(p), :]
    fp_copies[1].start()
    actsend[...] = active.astype(BF16)
    pending.extend(rm_copies)

    def owner_before(at):
        return lax.div(P // 2 + at, 2) <= z_at

    def to_owners(src_of, ref, sem, start=True):
        copies = []
        for at in range(4):
            target = P // 2 + at
            copy = pltpu.make_async_remote_copy(
                src_ref=src_of(at), dst_ref=ref.at[p], send_sem=sem.at[0, at],
                recv_sem=sem.at[1, p], device_id={"pix": target}, device_id_type=MESH,
            )
            copies.append(copy)

            @pl.when(p != target if start else (p != target) & owner_before(at))
            def _(copy=copy):
                copy.start()

            @pl.when(p == target)
            def _(at=at):
                ref[p] = src_of(at)[...]

        return copies

    act_copies = to_owners(lambda at: actsend, actrecv, act_sem)
    fc_copies = []
    for step in range(1, P):
        peer = lax.rem(p + step, P)
        copy = remote(fc_hi.at[:, fc_lanes(peer)], fcrecv.at[p], fc_sem, step - 1, "pix", peer)
        fc_copies.append((peer, copy))

        @pl.when(peer < p)
        def _(copy=copy):
            copy.start()

    fcrecv[p] = fc_hi[:, fc_lanes(p)]
    pending.extend(copy for _, copy in fc_copies)

    pfsend[0] = own_conv(core_peer).astype(BF16)
    pf_copies[0].start()

    arrive(rm_copies)
    for k in range(P // 2):
        even = rmrecv[64 * k : 64 * k + 32, :].astype(F32)
        odd = rmrecv[64 * k + 32 : 64 * k + 64, :].astype(F32)
        for jj in range(HJ):
            lanes = slice(128 * jj, 128 * (jj + 1))
            halves = unpack(even[:, lanes], odd[:, lanes])
            for half in range(2):
                j = jj + half * HJ
                for dy in range(3):
                    value = halves[half]
                    if dy > 0:
                        value = pltpu.roll(value, 8 * B - dy, 0)
                    if dy != 1:
                        value = value * mgrp[dy // 2]
                    for at in range(B):
                        fg[dy * lhs_rows + (at * J + j) * 8 : dy * lhs_rows + (at * J + j) * 8 + 8, 128 * k : 128 * (k + 1)] = (
                            value[8 * at : 8 * at + 8]
                        )
    for tap in range(9):
        loads[f"twu{tap}"].wait()
    block = J * 8
    per = 3 * block
    lhs = jnp.concatenate([fg[dy * lhs_rows : (dy + 1) * lhs_rows, :].astype(BF16) for dy in range(3)], axis=1)
    for dx in range(3):
        part = dot(lhs, twu[3 * dx : 3 * dx + 3].reshape(3 * C, C))
        for at in range(B):
            hsend[at * per + dx * block : at * per + (dx + 1) * block, :] = part[
                at * block : (at + 1) * block
            ].astype(BF16)

    def h_rows(at):
        return pl.ds(pl.multiple_of(at * per, per), per)

    h_copies = exchange("br", h_sem, lambda q: hsend.at[h_rows(q)], lambda me: hrecv.at[h_rows(me)])
    hrecv[h_rows(b), :] = hsend[h_rows(b), :]

    pre[...] = own_conv(b)
    pf_copies[0].wait_recv()
    pre[...] = pre[...] + pfrecv[0].astype(F32)

    def transpose_part(first, rows_of):
        def step(at, carry):
            values = rows_of(at).astype(F32)
            for dx in range(3):
                value = values if dx == 1 else shift_columns(values, dx - 1)
                fgrp[dx, first : first + half_c, pl.ds(pl.multiple_of(at * OPX, 128), OPX)] = turned(
                    value.astype(BF16)
                )
            return carry

        lax.fori_loop(0, B, step, 0)

    def my_features(at):
        rows = pl.ds(pl.multiple_of(W + at * OPX, W), OPX)
        return jnp.concatenate(
            [fext[rows, pl.ds(pl.multiple_of((x_at + 2 * z) * 128, 128), 128)] for z in range(2)], axis=1
        )

    def their_features(at):
        return jnp.concatenate(
            [upsend[pl.ds(pl.multiple_of(z * PX + at * OPX, W), OPX), :] for z in range(2)], axis=1
        )

    half_c = C // 2
    transpose_part(0, my_features)

    loads["x"].wait()
    arrive(pf_copies[2:])
    arrive(h_copies)
    pre[...] = pre[...] + pfrecv[2].astype(F32) + dot(xc[...], hrecv[...])

    def all_sum(value, send1, recv1, sem1, send2, recv2, sem2, first, second):
        send1[...] = value
        recv1[b] = value
        copies = exchange("br", sem1, lambda q: send1, lambda me: recv1.at[me])
        first()
        arrive(copies)
        pending.extend(copies)
        value = recv1[0]
        for at in range(1, B):
            value = value + recv1[at]
        send2[...] = value
        recv2[p] = value
        copies = exchange("pix", sem2, lambda q: send2, lambda me: recv2.at[me])
        second()
        arrive(copies)
        pending.extend(copies)
        value = recv2[0]
        for at in range(1, P):
            value = value + recv2[at]
        return value

    def row_sum(value):
        return jnp.sum(value, axis=0, keepdims=True)

    def tall_rows(rows):
        parts = [row[:, 128 * at : 128 * (at + 1)] for row in rows for at in range(row.shape[1] // 128)]
        parts.extend([jnp.zeros((1, 128), F32)] * (-len(parts) % 8))
        return jnp.concatenate(parts, axis=0)

    def wide_row(value, first, count):
        return jnp.concatenate([value[at : at + 1] for at in range(first, first + count)], axis=1)

    def turn_step(tap, carry):
        twf[tap] = turned(twf[tap])
        return carry

    lanes_c = C // 128
    whole = pre[...]
    stats = all_sum(
        tall_rows([row_sum(whole), row_sum(whole * whole)]),
        st1, sr1, st_sem1, st2, sr2, st_sem2,
        lambda: None, lambda: lax.fori_loop(0, 9, turn_step, 0),
    )
    total_pix = float(PX * P)
    t_mean = wide_row(stats, 0, lanes_c) / total_pix
    t_inv = lax.rsqrt(wide_row(stats, lanes_c, lanes_c) / total_pix - t_mean * t_mean + norm_eps)
    gain = tgain[...]
    shift = tshift[...]

    def norm_step(at, carry):
        rows = pl.ds(pl.multiple_of(at * W, W), W)
        hat = (pre[rows, :] - t_mean) * t_inv
        value, slope = gelu_parts(hat * gain + shift)
        hidden[rows, :] = value.astype(BF16)
        d_norm = dnorm[rows, :] * slope
        pre[rows, :] = hat
        dnorm[rows, :] = d_norm
        return carry[0] + row_sum(d_norm * hat), carry[1] + row_sum(d_norm)

    zero = jnp.zeros((1, C), F32)
    gain_sum, shift_sum = lax.fori_loop(0, Q, norm_step, (zero, zero))
    bias_sum = row_sum(lgp[...].astype(F32))
    def make_logits():
        logit = dot_nt(hidden[...], cwp[...])
        logits_out[...] = (logit[:, 0 : d.classes] + cbias[...]).astype(BF16)

    def make_class_grad():
        cwsend[...] = dot(turned(lgp[...])[0 : cwsend.shape[0]], hidden[...])
        for copy in fp_copies:
            copy.wait_recv()
        transpose_part(half_c, their_features)

    sums = all_sum(
        tall_rows([gain_sum, shift_sum, bias_sum]),
        st3, sr3, st_sem3, st4, sr4, st_sem4, make_logits, make_class_grad,
    )
    tot[...] = sums
    small_out[...] = jnp.zeros_like(small_out)
    small_out[2:3, 0 : C // B] = tot[pl.ds(b, 1), :]
    small_out[3:4, 0 : C // B] = tot[pl.ds(lanes_c + b, 1), :]
    small_out[4:5, 0:256] = wide_row(sums, 2 * lanes_c, 2)
    gain_mean = wide_row(sums, 0, lanes_c) / total_pix
    shift_mean = wide_row(sums, lanes_c, lanes_c) / total_pix

    def dp_rows(at):
        return pl.ds(pl.multiple_of(W + at * OPX, W), OPX)

    dpre = (gain * t_inv * (dnorm[...] - shift_mean - pre[...] * gain_mean)).astype(BF16)
    dpext[dp_rows(b), :] = dpre
    dp_core = remote(dpext.at[dp_rows(b)], dpext.at[dp_rows(b)], dp_sem, 0, "br", core_peer)
    dp_y = remote(dpext.at[dp_rows(b)], dpext.at[dp_rows(b)], dp_sem, 1, "br", y_peer)
    dp_on = remote(dpext.at[dp_rows(y_peer)], dpext.at[dp_rows(y_peer)], dp_sem, 2, "br", core_peer)
    dp_x = remote(dpext.at[dp_rows(b)], dpext2.at[dp_rows(b)], dp2_sem, 0, "pix", x_peer)
    pending.extend([dp_core, dp_y, dp_on, dp_x])
    dp_x.start()
    dp_core.start()
    dp_y.start()
    edge_copies = []
    for at in range(B):
        down = pltpu.make_async_remote_copy(
            src_ref=dpext.at[pl.ds(PX, W)], dst_ref=dpext.at[pl.ds(0, W)], send_sem=dphalo_sem.at[0, at],
            recv_sem=dphalo_sem.at[1, 0], device_id={"pix": lax.rem(p + 1, P), "br": at}, device_id_type=MESH,
        )
        up = pltpu.make_async_remote_copy(
            src_ref=dpext.at[pl.ds(W, W)], dst_ref=dpext.at[pl.ds(W + PX, W)], send_sem=dphalo_sem.at[0, at],
            recv_sem=dphalo_sem.at[1, 1], device_id={"pix": lax.rem(p + P - 1, P), "br": at}, device_id_type=MESH,
        )
        edge_copies.append((down, up))
    far_copies = []
    for at in range(B):
        down = pltpu.make_async_remote_copy(
            src_ref=dpext.at[pl.ds(PX, W)], dst_ref=dpext2.at[pl.ds(0, W)], send_sem=dphalo2_sem.at[0, at],
            recv_sem=dphalo2_sem.at[1, 0], device_id={"pix": lax.rem(p + 2, P), "br": at}, device_id_type=MESH,
        )
        up = pltpu.make_async_remote_copy(
            src_ref=dpext.at[pl.ds(W, W)], dst_ref=dpext2.at[pl.ds(W + PX, W)], send_sem=dphalo2_sem.at[0, at],
            recv_sem=dphalo2_sem.at[1, 0], device_id={"pix": lax.rem(p + P - 2, P), "br": at}, device_id_type=MESH,
        )
        far_copies.append((down, up))
    sends_far_down = (b == B - 1) & (x_at == 1) & (p < P - 2)
    sends_far_up = (b == 0) & (x_at == 0) & (p > 1)

    @pl.when(sends_far_down)
    def _():
        for down, up in far_copies:
            down.start()

    @pl.when(sends_far_up)
    def _():
        for down, up in far_copies:
            up.start()


    @pl.when((b == B - 1) & (p < P - 1))
    def _():
        for down, up in edge_copies:
            down.start()

    @pl.when((b == 0) & (p > 0))
    def _():
        for down, up in edge_copies:
            up.start()

    @pl.when(p == 0)
    def _():
        dpext[pl.ds(0, W), :] = jnp.zeros((W, C), BF16)

    @pl.when(p == P - 1)
    def _():
        dpext[pl.ds(W + PX, W), :] = jnp.zeros((W, C), BF16)


    for peer, copy in fc_copies:

        @pl.when(peer > p)
        def _(copy=copy):
            copy.start()

    def half_block(at, half):
        return pl.ds(pl.multiple_of(W + at * OPX + half * (OPX // 2), 32), OPX // 2)

    dp2_core = remote(dpext2.at[dp_rows(b)], dpext2.at[dp_rows(b)], dp2_sem, 1, "br", core_peer)
    dp2_x = remote(dpext.at[half_block(y_peer, 0)], dpext2.at[half_block(y_peer, 0)], dp2_sem, 2, "pix", x_peer)
    dp2_y = remote(dpext2.at[half_block(b, 1)], dpext2.at[half_block(b, 1)], dp2_sem, 3, "br", y_peer)
    dp2_on = [
        remote(dpext2.at[half_block(y_peer, n)], dpext2.at[half_block(y_peer, n)], dp2_sem, 4 + n, "br", core_peer)
        for n in range(2)
    ]
    pending.extend([dp2_core, dp2_x, dp2_y] + dp2_on)
    dp_x.wait_recv()
    dp2_y.start()
    dp2_core.start()
    dp_y.wait_recv()
    dp2_x.start()
    dp_on.start()

    cq = C // B

    def cq_lanes(at):
        return pl.ds(pl.multiple_of(at * cq, cq), cq)

    cw_copies1 = exchange(
        "br", cw_sem1, lambda q: cwsend.at[:, cq_lanes(q)], lambda me: cwr1.at[me]
    )
    cwr1[b] = cwsend[:, cq_lanes(b)]
    pending.extend(cw_copies1)

    dp_core.wait_recv()
    dp_on.wait_recv()

    @pl.when(p > 0)
    def _():
        edge_copies[0][0].wait_recv()

    @pl.when(p < P - 1)
    def _():
        edge_copies[0][1].wait_recv()

    loads["xt"].wait()
    own_columns = xt[h_rows(b), :]
    for at in range(B):
        drecv[at * per : (at + 1) * per, :] = dot(own_columns, dpext[W + at * OPX : W + (at + 1) * OPX, :]).astype(BF16)
    cols = []
    for dx in range(3):
        cols.append(
            jnp.concatenate(
                [drecv[at * per + dx * block : at * per + (dx + 1) * block, :] for at in range(B)], axis=0
            )
        )
    parts = []
    for dy in range(3):
        part = dot_nt(cols[0], twu[dy]) + dot_nt(cols[1], twu[3 + dy]) + dot_nt(cols[2], twu[6 + dy])
        if dy != 1:
            mask = jnp.concatenate(
                [mgrp[dy // 2, 8 * at : 8 * at + 8, :] for at in range(B) for j in range(J)], axis=0
            )
            part = part * jnp.concatenate([mask] * (C // 128), axis=1)
        if dy > 0:
            part = pltpu.roll(part, dy, 0)
        parts.append(part)
    d_mix = parts[0] + parts[1] + parts[2]

    def group_rows(value, j):
        return jnp.concatenate(
            [value[(at * J + j) * 8 : (at * J + j) * 8 + 8] for at in range(B)], axis=0
        )

    for k in range(P // 2):
        value = d_mix[:, 128 * k : 128 * (k + 1)]
        for jj in range(HJ):
            left, right = group_rows(value, jj), group_rows(value, jj + HJ)
            for odd in range(2):
                at = 32 * (2 * k + odd)
                drsend[at : at + 32, 128 * jj : 128 * (jj + 1)] = pack(left, right, odd).astype(BF16)
    dr_copies = exchange("pix", dr_sem, lambda q: drsend.at[rm_rows(q)], lambda me: drrecv.at[rm_rows(me)])
    drrecv[rm_rows(p), :] = drsend[rm_rows(p), :]
    pending.extend(dr_copies)

    def o_lanes(at):
        return pl.ds(at * 128, 128)

    def from_all(ref, sem, sources):
        for src in sources:

            @pl.when(p != src)
            def _(src=src):
                pltpu.make_async_remote_copy(
                    src_ref=ref.at[0], dst_ref=ref.at[src], send_sem=sem.at[0, 0],
                    recv_sem=sem.at[1, src], device_id={"pix": p}, device_id_type=MESH,
                ).wait_recv()

    dw_copies = to_owners(lambda at: drecv.at[:, o_lanes(at)], dwrecv, dw_sem, start=False)

    shift_rows(dpext, mrow, backward_lanes)
    half_rows = C // 4

    def tap_product(tap, first):
        dy, dx = lax.div(tap, 3), lax.rem(tap, 3)
        return dot(fgrp[dx, first : first + half_c, 0:PX], shifted[:, pl.ds(pl.multiple_of((2 - dy) * C, C), C)])

    def own_step(tap, carry):
        keep[tap] = tap_product(tap, 0)
        return carry

    lax.fori_loop(0, 5, own_step, 0)
    dp2_x.wait_recv()
    dp2_on[0].start()
    dp2_y.wait_recv()
    dp2_on[1].start()
    lax.fori_loop(5, 9, own_step, 0)

    arrive(cw_copies1)
    cw2[...] = cwr1[0] + cwr1[1] + cwr1[2] + cwr1[3]
    c_part = cwsend.shape[0] // P

    def cw_rows(at):
        return pl.ds(pl.multiple_of(at * c_part, 8), c_part)

    cw_copies2 = exchange("pix", cw_sem2, lambda q: cw2.at[cw_rows(q)], lambda me: cwr2.at[me])
    cwr2[p] = cw2[cw_rows(p), :]
    pending.extend(cw_copies2)

    arrive(dr_copies)
    d_active = jnp.dot(mix_t[...], drrecv[...].astype(F32), precision=HIGH, preferred_element_type=F32)
    hat = bhat[...]
    d_normed = d_active * valid_f * gelu_parts(bnorm[...])[1]
    gain_part = over_bins(d_normed * hat)
    shift_part = over_bins(d_normed)
    scale = thrice(own_channels(bgain) * binv[0:1])
    d_pooled = scale * (d_normed - thrice(shift_part / total_bins) - hat * thrice(gain_part / total_bins)) * valid_f
    dssend[...] = (d_pooled / count).astype(BF16)
    dsrecv[p] = dssend[...]
    ds_copies = []
    for step in range(1, P // 2):
        copy = remote(dssend, dsrecv.at[p], ds_sem, step - 1, "pix", lax.rem(p + 2 * step, P))
        copy.start()
        ds_copies.append(copy)
    ds_across = []
    for step in range(P // 2):
        at = lax.rem(p + P - 2 * step, P)
        ds_across.append(remote(dsrecv.at[at], dsrecv.at[at], ds_sem, P // 2 - 1 + step, "pix", x_peer))
    ds_across[0].start()
    small = jnp.concatenate([gain_part, shift_part, jnp.zeros((6, 128), F32)], axis=0)
    smsend[...] = small
    sm_copies = exchange("pix", sm_sem, lambda q: smsend, lambda me: smrecv.at[me])
    smrecv[p] = small
    pending.extend(ds_copies + ds_across + sm_copies)

    for at in range(4):

        @pl.when((p != P // 2 + at) & jnp.logical_not(owner_before(at)))
        def _(at=at):
            dw_copies[at].start()

    @pl.when(x_at == 0)
    def _():
        dpext2[pl.ds(0, W), :] = dpext[pl.ds(PX, W), :]

    @pl.when(x_at == 1)
    def _():
        dpext2[pl.ds(W + PX, W), :] = dpext[pl.ds(W, W), :]

    @pl.when(p == 1)
    def _():
        dpext2[pl.ds(0, W), :] = jnp.zeros((W, C), BF16)

    @pl.when(p == P - 2)
    def _():
        dpext2[pl.ds(W + PX, W), :] = jnp.zeros((W, C), BF16)

    @pl.when((x_at == 1) & (p > 1))
    def _():
        far_copies[0][0].wait_recv()

    @pl.when((x_at == 0) & (p < P - 2))
    def _():
        far_copies[0][1].wait_recv()

    dp2_core.wait_recv()
    arrive(dp2_on)
    shift_rows(dpext2, mrow2, backward_lanes)

    def half_of(half):
        return pl.ds(half * half_rows, half_rows)

    def z_copy(tap, half):
        rows = half_of(half)
        return remote(
            sendx.at[tap, rows], recvz.at[tap, rows], zz_sem, tap * 2 + half, "pix", lax.rem(p + P - 2, P)
        )

    def a_rows(tap):
        return pl.ds(pl.multiple_of(lax.rem(tap, 3) * half_rows, 128), half_rows)

    def a_copy(tap):
        rows = pl.ds(pl.multiple_of((1 - z_at) * half_rows, 128), half_rows)
        return remote(sendx.at[tap, rows], pfrecv.at[lax.div(tap, 3), a_rows(tap)], a_sem, tap, "pix", lax.rem(p + 2 - 4 * z_at + 2 * P, P))

    def twg_copy(tap):
        return pltpu.make_async_copy(recvz.at[tap, half_of(0)], twg_hbm.at[tap], twg_sem.at[tap])

    def finish(tap):
        a_copy(tap).wait_recv()
        rows = pl.ds(pl.multiple_of(z_at * half_rows, 128), half_rows)
        recvz[tap, 0:half_rows, :] = (
            keep[tap, rows, :] + pfrecv[lax.div(tap, 3), a_rows(tap), :].astype(F32)
        ).astype(BF16)

    def peer_step(tap, carry):
        keep[tap] = keep[tap] + tap_product(tap, half_c)

        @pl.when((z_at == 0) | (z_at == 3))
        def _():
            sendx[tap] = keep[tap].astype(BF16)

        @pl.when(z_at == 3)
        def _():
            z_copy(tap, 0).start()
            z_copy(tap, 1).start()

        @pl.when(z_at == 0)
        def _():
            a_copy(tap).start()

        return carry

    lax.fori_loop(0, 9, peer_step, 0)

    def chain_step(tap, carry):
        @pl.when((z_at == 1) | (z_at == 2))
        def _():
            for half in range(2):
                z_copy(tap, half).wait_recv()
                rows = half_of(half)
                keep[tap, rows, :] = keep[tap, rows, :] + recvz[tap, rows, :].astype(F32)
                if half == 0:
                    sendx[tap, rows, :] = keep[tap, rows, :].astype(BF16)

                    @pl.when(z_at == 2)
                    def _():
                        z_copy(tap, 0).start()

                    @pl.when(z_at == 1)
                    def _():
                        a_copy(tap).start()

                else:

                    @pl.when(z_at == 2)
                    def _():
                        sendx[tap, rows, :] = keep[tap, rows, :].astype(BF16)
                        z_copy(tap, 1).start()

        return carry

    def chain_to(tap):
        lax.fori_loop(tap, tap + 1, chain_step, 0)

    chain_to(0)
    for step in range(1, P // 2):
        ds_copies[step - 1].wait_recv()
        ds_across[step].start()


    def unpack_all(source, target):
        for k in range(P // 2):
            even = source[2 * k].astype(F32)
            odd = source[2 * k + 1].astype(F32)
            for jj in range(HJ):
                lanes = slice(128 * jj, 128 * (jj + 1))
                halves = unpack(even[:, lanes], odd[:, lanes])
                for half in range(2):
                    j = jj + half * HJ
                    target[j * NB : (j + 1) * NB, 128 * k : 128 * (k + 1)] = halves[half].astype(BF16)

    arrive(cw_copies2)
    value = cwr2[0]
    for at in range(1, P):
        value = value + cwr2[at]
    cw3[...] = value
    cw_copies3 = exchange("pix", cw_sem3, lambda q: cw3, lambda me: cwr3.at[cw_rows(me)])
    cwr3[cw_rows(p), :] = value
    pending.extend(cw_copies3)

    chain_to(1)
    arrive(ds_across)
    unpack_all(dsrecv, ds_all)
    hot_mine = hot_own[...].astype(BF16)
    d_col = [dot(hot_mine, ds_all[j * NB : (j + 1) * NB, :]) for j in range(J)]
    d_col = jnp.concatenate(
        [d_col[j][8 * g : 8 * g + 8] for g in range(groups) for j in range(J)], axis=0
    ).astype(BF16)
    esend[...] = dot_nt(d_col, wb[...]).astype(BF16)

    def e_lanes(at):
        return pl.ds(pl.multiple_of(at * C, C), C)

    e_copies = exchange("br", e_sem, lambda q: esend.at[:, e_lanes(q)], lambda me: erecv.at[me])
    erecv[b] = esend[:, e_lanes(b)]
    pending.extend(e_copies)

    chain_to(2)
    shift_rows(dpext, mrow, backward_lanes)
    def back_step(at, carry):
        fg[pf_rows(at), :] = conv_chunk(at, -1)
        return carry

    lax.fori_loop(0, B // 2, back_step, 0)
    chain_to(3)
    lax.fori_loop(B // 2, B, back_step, 0)
    chain_to(4)
    for copy in pf_copies + h_copies:
        copy.wait_send()
    up_copies = []
    up_rows = 9 * 128
    for at in range(4):
        target = P // 2 + at
        up_copies.append(
            pltpu.make_async_remote_copy(
                src_ref=upsend.at[pl.ds(at * up_rows, up_rows)], dst_ref=uprecv.at[lax.rem(p, P // 2)], send_sem=up_sem.at[0, at],
                recv_sem=up_sem.at[1, p], device_id={"pix": target}, device_id_type=MESH,
            )
        )

    @pl.when(z_at >= 2)
    def _():
        from_all(actrecv, act_sem, range(P))
        unpack_all(actrecv, hsend)
        from_all(dwrecv, dw_sem, range(P))
        k_rows = P * B * block
        for dx in range(3):
            value = jnp.concatenate(
                [
                    dwrecv[at, per * owner + block * dx : per * owner + block * (dx + 1), :]
                    for at in range(P)
                    for owner in range(B)
                ],
                axis=0,
            )
            value = turned(value)
            for part in range(k_rows // C):
                pfsend[part, 128 * dx : 128 * (dx + 1), :] = value[:, C * part : C * (part + 1)]
        t_grp, k_grp = halo_rows((8 * B * P, 1), 0, 0)
        here_grp = jnp.where(k_grp < Q, row_info(t_grp)[0], -3)

        def up_step(dy, carry):
            mix = row_mix(t_grp + (dy - 1), g_row, i_row, here_grp)
            mix_high = mix.astype(BF16)
            mix_low = (mix - mix_high.astype(F32)).astype(BF16)
            for pair in range(J // 2):
                two = []
                for j in (2 * pair, 2 * pair + 1):
                    act = hsend[j * NB : (j + 1) * NB, :]
                    two.append(dot(mix_high, act) + dot(mix_low, act))
                for at in range(P * B):
                    value = jnp.concatenate([rows[8 * at : 8 * at + 8] for rows in two], axis=0)
                    to = at * block + 16 * pair
                    fgrp[to // C, to % C : to % C + 16, 0:C] = value.astype(BF16)
            total = None
            for part in range(k_rows // C):
                term = dot(pfsend[part], fgrp[part, 0:C, 0:C])
                total = term if total is None else total + term
            for at in range(4):
                upsend[pl.ds(pl.multiple_of(at * up_rows + dy * 384, 128), 384), :] = total[
                    :, 128 * at : 128 * (at + 1)
                ].astype(BF16)
            return carry

        lax.fori_loop(0, 3, up_step, 0)
        for at, copy in enumerate(up_copies):

            @pl.when(p != P // 2 + at)
            def _(copy=copy):
                copy.start()

            @pl.when(p == P // 2 + at)
            def _(at=at):
                uprecv[at] = upsend[at * up_rows : (at + 1) * up_rows, :]

    chain_to(5)
    arrive([copy for _, copy in fc_copies])
    hot16 = hot_all[...].astype(BF16)

    def eight(at, row):
        pair = fcrecv[at, row // 16 * 16 : row // 16 * 16 + 16, :].astype(F32)
        return pair[row % 16 : row % 16 + 8]

    for j in range(J):
        rows = jnp.concatenate(
            [eight(at, (g * J + j) * 8) for at in range(P) for g in range(groups)],
            axis=0,
        )
        fp_all[j * NB : (j + 1) * NB, :] = dot(hot16, rows.astype(BF16)).astype(BF16)
    fp_t[...] = turned(fp_all[...])

    bwg_out[...] = dot(fp_t[...], ds_all[...])
    arrive(sm_copies)
    for k in range(P // 2):
        lanes = slice(128 * k, 128 * (k + 1))
        is_low = low((1, 128))
        small_out[0:1, lanes] = jnp.where(is_low, smrecv[2 * k, 0:1, :], smrecv[2 * k + 1, 0:1, :])
        small_out[1:2, lanes] = jnp.where(is_low, smrecv[2 * k, 1:2, :], smrecv[2 * k + 1, 1:2, :])

    chain_to(6)
    arrive(e_copies)
    loads["spread"].wait()
    for g in range(groups):
        rows = jnp.concatenate([erecv[at, block * g : block * (g + 1), :] for at in range(B)], axis=0)
        total = fg[gpx * g : gpx * (g + 1), :] + dot(spread8[...], rows)
        shifted[gpx * g : gpx * (g + 1), 0:C] = total.astype(BF16)
    fg_copy = pltpu.make_async_copy(shifted.at[:, pl.ds(0, C)], fg_hbm, out_sem.at[0])
    fg_copy.start()

    chain_to(7)

    @pl.when(z_at < 2)
    def _():
        def most(tap, carry):
            finish(tap)
            twg_copy(tap).start()
            return carry

        lax.fori_loop(0, 7, most, 0)

    chain_to(8)

    @pl.when(z_at < 2)
    def _():
        def last(tap, carry):
            finish(tap)
            twg_copy(tap).start()
            return carry

        lax.fori_loop(7, 9, last, 0)

    @pl.when(z_at >= 2)
    def _():
        for src in range(4):

            @pl.when(p != P // 2 + src)
            def _(src=src):
                pltpu.make_async_remote_copy(
                    src_ref=upsend.at[pl.ds(0, up_rows)], dst_ref=uprecv.at[src], send_sem=up_sem.at[0, 0],
                    recv_sem=up_sem.at[1, P // 2 + src], device_id={"pix": p}, device_id_type=MESH,
                ).wait_recv()

        def gather(tap, carry):
            rows = pl.ds(pl.multiple_of(tap * 128, 128), 128)
            value = jnp.concatenate([uprecv[at, rows, :] for at in range(4)], axis=0)
            recvz[tap, 0:half_rows, :] = turned(value)
            twg_copy(tap).start()
            return carry

        lax.fori_loop(0, 9, gather, 0)

    arrive(cw_copies3)
    cwg_out[...] = cwr3[0 : d.classes, :]

    pending.extend(fp_copies)

    for copy in pending:
        copy.wait_send()

    @pl.when(p < P - 1)
    def _():
        halo_down.wait_send()

    @pl.when(p > 0)
    def _():
        halo_up.wait_send()

    @pl.when((b == B - 1) & (p < P - 1))
    def _():
        for down, up in edge_copies:
            down.wait_send()

    @pl.when((b == 0) & (p > 0))
    def _():
        for down, up in edge_copies:
            up.wait_send()

    @pl.when(sends_far_down)
    def _():
        for down, up in far_copies:
            down.wait_send()

    @pl.when(sends_far_up)
    def _():
        for down, up in far_copies:
            up.wait_send()

    for at in range(4):

        @pl.when(p != P // 2 + at)
        def _(at=at):
            dw_copies[at].wait_send()
            act_copies[at].wait_send()

        @pl.when((z_at >= 2) & (p != P // 2 + at))
        def _(at=at):
            up_copies[at].wait_send()

    def sent(tap, carry):
        @pl.when(z_at >= 2)
        def _():
            z_copy(tap, 0).wait_send()
            z_copy(tap, 1).wait_send()

        @pl.when(z_at < 2)
        def _():
            a_copy(tap).wait_send()

        return carry

    lax.fori_loop(0, 9, sent, 0)
    fg_copy.wait()

    def handed(tap, carry):
        twg_copy(tap).wait()
        return carry

    lax.fori_loop(0, 9, handed, 0)


def spread_tables(width, own, rows):
    side = max(bin_sides)
    count = len(bin_sides)
    cols = shifted_columns(bin_sides, width, side)
    up = np.zeros((own, width, count, 3, side, 8), np.float32)
    for m in range(own):
        up[m, :, :, :, :, m] = cols.transpose(2, 0, 1, 3)
    up = up.reshape(own * width, count * 3 * side * 8)
    bins = column_bins(bin_sides, width, side)
    pool = np.zeros((count, side, 8, 8, width), np.float32)
    spread = np.zeros((8, width, count, side, 8), np.float32)
    for r in range(8):
        pool[:, :, r, r, :] = bins
        spread[r, :, :, :, r] = bins.transpose(2, 0, 1)
    bf16 = jnp.bfloat16
    return (
        jnp.asarray(up, bf16),
        jnp.asarray(up.T, bf16),
        jnp.asarray(pool.reshape(count, side * 8, 8 * width), bf16),
        jnp.asarray(spread.reshape(8 * width, count * side * 8), bf16),
    )


def on_device_fused(
    features,
    branch_weight,
    branch_gain,
    branch_shift,
    trunk_weight,
    trunk_gain,
    trunk_shift,
    class_weight,
    class_bias,
    heights,
    logit_grad,
):
    P, B = lax.axis_size("pix"), lax.axis_size("br")
    d = Shape(features, branch_weight, class_weight, heights, P, B)
    W, C, J, NB, R, PX, OPX = d.width, d.ch, d.side, d.bins, d.rows, d.px, d.own_px
    CH, K = d.channels, d.classes
    per = 3 * J * 8
    groups = R // 8
    up, up_t, pool, spread = spread_tables(W, d.own, R)
    half = C // 4
    kp = -(-K // (8 * P)) * 8 * P
    vmem, sem = pltpu.VMEM, pltpu.SemaphoreType.DMA
    scratch = dict(
        fext=vmem((PX + 2 * W, C), BF16), shifted=vmem((PX, 3 * C), BF16), fgrp=vmem((groups, 8 * W, CH), BF16),
        wb=vmem((CH, C), BF16), twf=vmem((9, C, C), BF16), twu=vmem((9, C, C), BF16),
        xc=vmem(up.shape, BF16), xt=vmem(up_t.shape, BF16), pool8=vmem(pool.shape[1:], BF16), spread8=vmem(spread.shape, BF16),
        fc_hi=vmem((groups * J * 8, CH), BF16), zsend=vmem((P, R, 384), F32), zrecv=vmem((P * R, 384), F32),
        fcrecv=vmem((P, groups * J * 8, CH // P), BF16), pfsend=vmem((B - 1, OPX, C), BF16), pfrecv=vmem((B - 1, OPX, C), BF16),
        hidden=vmem((OPX, C), BF16),
        hot_all=vmem((NB, P * R), F32), mix_all=vmem((8 * B * P, NB), F32), mix_t=vmem((NB, 8 * B * P), F32), hot_own=vmem((R, NB), F32),
        mrow=vmem((2, 32, 128), F32), mrow2=vmem((2, 32, 128), F32), mgrp=vmem((2, 8 * B, 128), F32),
        bhat=vmem((NB, 384), F32), bnorm=vmem((NB, 384), F32), binv=vmem((8, 128), F32),
        rmsend=vmem((8 * B * P, 384), BF16), rmrecv=vmem((8 * B * P, 384), BF16), actsend=vmem((NB, 384), BF16), actrecv=vmem((P, NB, 384), BF16),
        hsend=vmem((B * per, C), BF16), hrecv=vmem((B * per, C), BF16),
        st1=vmem((8, 128), F32), st2=vmem((8, 128), F32), st3=vmem((16, 128), F32), st4=vmem((16, 128), F32),
        sr1=vmem((B, 8, 128), F32), sr2=vmem((P, 8, 128), F32), sr3=vmem((B, 16, 128), F32), sr4=vmem((P, 16, 128), F32), tot=vmem((16, 128), F32),
        cwp=vmem((256, C), BF16), lgp=vmem((OPX, 256), BF16), cwsend=vmem((kp, C), F32), cwr1=vmem((B, kp, C // B), F32),
        cw2=vmem((kp, C // B), F32), cwr2=vmem((P, kp // P, C // B), F32), cw3=vmem((kp // P, C // B), F32), cwr3=vmem((kp, C // B), F32),
        dpext=vmem((PX + 2 * W, C), BF16), dpext2=vmem((PX + 2 * W, C), BF16), drecv=vmem((B * per, C), BF16),
        drsend=vmem((8 * B * P, 384), BF16), drrecv=vmem((8 * B * P, 384), BF16),
        dwrecv=vmem((P, B * per, 128), BF16),
        dssend=vmem((NB, 384), BF16), dsrecv=vmem((P, NB, 384), BF16), smsend=vmem((8, 128), F32), smrecv=vmem((P, 8, 128), F32),
        ds_all=vmem((J * NB, C), BF16), fp_all=vmem((J * NB, CH // P), BF16), fp_t=vmem((CH // P, J * NB), BF16), esend=vmem((groups * J * 8, CH), BF16),
        erecv=vmem((B, groups * J * 8, C), BF16), fg=vmem((PX, C), F32), keep=vmem((9, 2 * half, C), F32),
        sendx=vmem((9, 2 * half, C), BF16),
        recvz=vmem((9, 2 * half, C), BF16),
        upsend=vmem((4 * 9 * 128, 128), BF16), uprecv=vmem((4, 9 * 128, 128), BF16), eye=vmem((C, C), BF16),
        load_sem=sem((27,)), out_sem=sem((2,)), twg_sem=sem((9,)), halo_sem=sem((2, 2)), z_sem=sem((2, P)), fc_sem=sem((2, P)), pf_sem=sem((2, B)),
        rm_sem=sem((2, P)), act_sem=sem((2, P)), h_sem=sem((2, B)),
        st_sem1=sem((2, B)), st_sem2=sem((2, P)), st_sem3=sem((2, B)), st_sem4=sem((2, P)),
        cw_sem1=sem((2, B)), cw_sem2=sem((2, P)), cw_sem3=sem((2, P)),
        dp_sem=sem((2, B)), dphalo_sem=sem((2, B)), dp2_sem=sem((2, 6)), dphalo2_sem=sem((2, B)), fp_sem=sem((2, 2)), dr_sem=sem((2, P)), dw_sem=sem((2, P)), ds_sem=sem((2, P)),
        sm_sem=sem((2, P)), e_sem=sem((2, B)), zz_sem=sem((2, 24)), a_sem=sem((2, 9)), up_sem=sem((2, P)),
    )
    hbm = pl.BlockSpec(memory_space=pl.ANY)
    local = pl.BlockSpec(memory_space=pltpu.VMEM)
    scalars = pl.BlockSpec(memory_space=pltpu.SMEM)

    def out(shape, dtype):
        return jax.ShapeDtypeStruct(shape, dtype)

    outs = pl.pallas_call(
        functools.partial(fused_kernel, d),
        out_shape=(
            out((OPX, K), BF16), out((PX, C), BF16), out((CH // P, C), F32), out((9, half, C), BF16),
            out((K, C // B), F32), out((8, C), F32),
        ),
        in_specs=[hbm] * 7 + [local] * 7 + [scalars],
        out_specs=(local, hbm, local, hbm, local, local),
        scratch_shapes=list(scratch.values()),
        compiler_params=pltpu.CompilerParams(
            collective_id=0, has_side_effects=True, vmem_limit_bytes=127 * 512 * 1024
        ),
    )(
        features.reshape(PX, CH), branch_weight[0], trunk_weight.reshape(9, 2 * C, C), up, up_t, pool, spread,
        branch_gain, branch_shift, trunk_gain[None], trunk_shift[None], class_weight.T, class_bias[None],
        logit_grad.reshape(OPX, K), heights,
    )

    def hand_on(*refs):
        src, small, dst, smalls = refs[:5], refs[5], refs[6:11], refs[11:16]
        held, wide, sems = refs[16:21], {1: refs[21], 3: refs[22]}, refs[23]
        parts = []
        for at in (1, 3, 0, 2, 4):
            rows = src[at].shape[0]
            cuts = {1: 8, 3: 9}.get(at, 1)
            for cut in range(cuts):
                part = pl.ds(cut * (rows // cuts), rows // cuts)
                n = len(parts)
                parts.append(
                    (
                        at,
                        part,
                        pltpu.make_async_copy(src[at].at[part], held[at].at[part], sems.at[0, n]),
                        pltpu.make_async_copy(wide.get(at, held[at]).at[part], dst[at].at[part], sems.at[1, n]),
                    )
                )
        for _, _, there, _ in parts:
            there.start()
        for at, ref in enumerate(smalls):
            ref[...] = small[at : at + 1, 0 : ref.shape[1]]
        for at, part, there, back in parts:
            there.wait()
            if at in wide:
                wide[at][part] = held[at][part].astype(F32)
            back.start()
        for _, _, _, back in parts:
            back.wait()

    logits, fg, bwg, twg, cwg, bgg, bsg, tgg, tsg, cbg = pl.pallas_call(
        hand_on,
        out_shape=tuple(out(o.shape, BF16 if at == 0 else F32) for at, o in enumerate(outs[:5]))
        + tuple(out((1, n), F32) for n in (C, C, C // B, C // B, K)),
        in_specs=[hbm] * 5 + [local],
        out_specs=tuple([hbm] * 5 + [local] * 5),
        scratch_shapes=[vmem(o.shape, o.dtype) for o in outs[:5]]
        + [vmem(outs[1].shape, F32), vmem(outs[3].shape, F32), sem((2, 24))],
        compiler_params=pltpu.CompilerParams(vmem_limit_bytes=127 * 512 * 1024),
    )(*outs)
    return (
        logits.reshape(d.own, W, K), fg.reshape(R, W, C), bwg[None], bgg, bsg,
        twg.reshape(1, 3, 3, half, C), tgg[0], tsg[0], cwg.T, cbg[0],
    )


def solution(mesh):
    in_specs = (
        P("pix", None, None),
        P("br", None, None),
        P("br", None),
        P("br", None),
        P("br", None, None, None, None),
        P(),
        P(),
        P(),
        P(),
        P(),
        P(("pix", "br"), None, None),
    )
    out_specs = (
        P(("pix", "br"), None, None),
        P("pix", None, "br"),
        P("br", "pix", None),
        P("br", None),
        P("br", None),
        P("br", None, None, "pix", None),
        P("br"),
        P("br"),
        P("br", None),
        P(),
    )
    fused = mesh.shape["pix"] == 8 and mesh.shape["br"] == 4
    return jax.shard_map(
        on_device_fused if fused else on_device, mesh=mesh, in_specs=in_specs, out_specs=out_specs, check_vma=False
    )
```

time: 956 us -> 173 us (0.18)
  waiting for transfers between devices: 637 us -> 0 us
  Pallas kernels: 0 us -> 172 us
  matrix products: 145 us -> 0 us
  other arithmetic: 55.8 us -> 0 us
  local copies, waits for them, and re-layouts: 44 us -> 0 us
  blocking collectives: 38.2 us -> 0 us
  between operations: 18 us -> 0.84 us
  starting transfers between devices: 11.8 us -> 0 us
    reduce_scatter x5 -> x0, waiting for transfers between devices: 458 us -> none  [the longest x1 314 us: on_device(): lax.psum_scatter(weight_term, 'pix', scatter_dimension=3, tiled=True)]
    pallas_call x0 -> x2, Pallas kernels: none -> 172 us  [the longest x1 167 us: on_device_fused(): pl.pallas_call(functools.partial(fused_kernel, d), out_shape=(out((OPX, K...]
    psum x2 -> x0, waiting for transfers between devices: 146 us -> none  [the longest x1 79.8 us: on_device(): lax.psum(d_bin_part, 'pix').reshape(images, most_side, most_side, branch_ch)]
    dot_general x40 -> x0, matrix products: 145 us -> none  [the longest x22 97.2 us: contract(): lax.dot_general(left, right, (((left_dim,), (right_dim,)), ((), ())), pre...]
    all_gather x1 -> x0, waiting for transfers between devices: 29.3 us -> none  [on_device(): d_summed = lax.all_gather(d_share, 'br', axis=2, tiled=True)]
    psum x2 -> x0, blocking collectives: 27.8 us -> none  [the longest x1 15.9 us: on_device(): lax.psum((weight_part, bias_part, gain_part, shift_part), 'pix')]
    reduce_sum x14 -> x0, other arithmetic: 16.2 us -> none  [the longest x2 3.75 us: on_device(): branch_shift_part = jnp.sum(d_normed, axis=(0, 1, 2))]
    unnamed x95 -> x0, local copies, waits for them, and re-layouts: 14.2 us -> none
  transfers between devices with their start and end apart: 12 -> 0, of which waited for: 9 -> 0; matrix products, arithmetic and copies ran while one was open for 9% -> 0% of each run, Pallas kernels for 0% -> 0%
where the time goes in v1:
time: 173 us
  Pallas kernels  172 us (99%)
    pallas_call x1, Pallas kernels, on_device_fused(): pl.pallas_call(functools.partial(fused_kernel, d), out_shape=(out((OPX, K...  167 us
    pallas_call x1, Pallas kernels, on_device_fused(): pl.pallas_call(hand_on, out_shape=tuple((out(o.shape, BF16 if at == 0 els...  5.31 us

profile of v1, /device:TPU:23, one launch (start us, length us, event | category | flops | bytes accessed | tf_op | source)
XLA Modules:
  0.0 172.7 jit_solution(4392015069636375445)
XLA Ops:
  0.6 166.5 %shard_map.222 = (bf16[384,150]{1,0:T(8,128)(2,1)}, bf16[1536,512]{1,0:T(8,128)(2,1)}, f32[256,512]{1,0:T(8,128)}, bf16[9,128,512]{2,1,0:T(8,128)(2,1)}, f32[150,128]{1,0:T(8,128)}, /*index=5*/f32[8,512]{1,0:T(8,128)}) custom-call(bf16[1536,2048]{1,0:T(8,128)(2,1)} %bitcast.17, bf16[2048,512]{1,0:T(8,128)(2,1)} %bitcast.18, bf16[9,1024,512]{2,1,0:T(8,128)(2,1)} %bitcast.16, ...), custom_call_target="tpu_custom_call" | custom-call | tf_op jit(solution)/shard_map/pallas_call | solution.py:1619
  167.2 5.3 %shard_map.223 = (bf16[384,150]{1,0:T(8,128)(2,1)}, f32[1536,512]{1,0:T(8,128)}, f32[256,512]{1,0:T(8,128)}, f32[9,128,512]{2,1,0:T(8,128)}, f32[150,128]{1,0:T(...) custom-call(bf16[384,150]{1,0:T(8,128)(2,1)} %get-tuple-element.26.r, ...), custom_call_target="tpu_custom_call" | custom-call | tf_op jit(solution)/shard_map/pallas_call | solution.py:1667

commit v2 on v1

--- a/solution.py
+++ b/solution.py
@@ -738,7 +738,18 @@
     def owner_before(at):
         return lax.div(P // 2 + at, 2) <= z_at
 
-    def to_owners(src_of, ref, sem, start=True):
+    def in_column_order(copies, wanted=None):
+        for column in range(2):
+            for at, copy in enumerate(copies):
+                go = (p != P // 2 + at) & (lax.rem(x_at + column, 2) == at % 2)
+                if wanted is not None:
+                    go = go & wanted(at)
+
+                @pl.when(go)
+                def _(copy=copy):
+                    copy.start()
+
+    def to_owners(src_of, ref, sem, only_before=False):
         copies = []
         for at in range(4):
             target = P // 2 + at
@@ -748,14 +759,11 @@
             )
             copies.append(copy)
 
-            @pl.when(p != target if start else (p != target) & owner_before(at))
-            def _(copy=copy):
-                copy.start()
-
             @pl.when(p == target)
             def _(at=at):
                 ref[p] = src_of(at)[...]
 
+        in_column_order(copies, owner_before if only_before else None)
         return copies
 
     act_copies = to_owners(lambda at: actsend, actrecv, act_sem)
@@ -1098,7 +1106,7 @@
                     recv_sem=sem.at[1, src], device_id={"pix": p}, device_id_type=MESH,
                 ).wait_recv()
 
-    dw_copies = to_owners(lambda at: drecv.at[:, o_lanes(at)], dwrecv, dw_sem, start=False)
+    dw_copies = to_owners(lambda at: drecv.at[:, o_lanes(at)], dwrecv, dw_sem, only_before=True)
 
     shift_rows(dpext, mrow, backward_lanes)
     half_rows = C // 4
@@ -1155,11 +1163,7 @@
     smrecv[p] = small
     pending.extend(ds_copies + ds_across + sm_copies)
 
-    for at in range(4):
-
-        @pl.when((p != P // 2 + at) & jnp.logical_not(owner_before(at)))
-        def _(at=at):
-            dw_copies[at].start()
+    in_column_order(dw_copies, lambda at: jnp.logical_not(owner_before(at)))
 
     @pl.when(x_at == 0)
     def _():
@@ -1376,11 +1380,8 @@
             return carry
 
         lax.fori_loop(0, 3, up_step, 0)
-        for at, copy in enumerate(up_copies):
-
-            @pl.when(p != P // 2 + at)
-            def _(copy=copy):
-                copy.start()
+        in_column_order(up_copies)
+        for at in range(4):
 
             @pl.when(p == P // 2 + at)
             def _(at=at):

time: 173 us -> 173 us (level)
  no operation moved by 1% of the time
where the time goes in v2:
time: 173 us
  Pallas kernels  172 us (99%)
    pallas_call x1, Pallas kernels, on_device_fused(): pl.pallas_call(functools.partial(fused_kernel, d), out_shape=(out((OPX, K...  166 us
    pallas_call x1, Pallas kernels, on_device_fused(): pl.pallas_call(hand_on, out_shape=tuple((out(o.shape, BF16 if at == 0 els...  5.31 us

profile of v2, /device:TPU:23, one launch (start us, length us, event | category | flops | bytes accessed | tf_op | source)
XLA Modules:
  0.0 172.6 jit_solution(2489081018353990027)
XLA Ops:
  0.6 166.5 %shard_map.222 = (bf16[384,150]{1,0:T(8,128)(2,1)}, bf16[1536,512]{1,0:T(8,128)(2,1)}, f32[256,512]{1,0:T(8,128)}, bf16[9,128,512]{2,1,0:T(8,128)(2,1)}, f32[150,128]{1,0:T(8,128)}, /*index=5*/f32[8,512]{1,0:T(8,128)}) custom-call(bf16[1536,2048]{1,0:T(8,128)(2,1)} %bitcast.17, bf16[2048,512]{1,0:T(8,128)(2,1)} %bitcast.18, bf16[9,1024,512]{2,1,0:T(8,128)(2,1)} %bitcast.16, ...), custom_call_target="tpu_custom_call" | custom-call | tf_op jit(solution)/shard_map/pallas_call | solution.py:1620
  167.1 5.3 %shard_map.223 = (bf16[384,150]{1,0:T(8,128)(2,1)}, f32[1536,512]{1,0:T(8,128)}, f32[256,512]{1,0:T(8,128)}, f32[9,128,512]{2,1,0:T(8,128)}, f32[150,128]{1,0:T(...) custom-call(bf16[384,150]{1,0:T(8,128)(2,1)} %get-tuple-element.26.r, ...), custom_call_target="tpu_custom_call" | custom-call | tf_op jit(solution)/shard_map/pallas_call | solution.py:1668
